TPU v7x, 32 devices: a whole 2x2x4 slice. The times are simulated.
32 devices in a mesh: region: 8 (over z, x), chan: 4 (over y, core).
Axes of the slice: x: 2, y: 2, z: 4, core: 2. Of those that a mesh axis runs over, the one named last changes fastest.
Arguments:
- point_feats: bfloat16 [64, 131072], P('chan', 'region'), may hold values from -6 to 6
- destination: int32 [131072], P('region'), may hold values from 0 to 7, as said below
- voxel_slot: int32 [131072], P('region'), may hold values from 0 to 32767, as said below
- adjacency: int32 [512, 26], P('region'), may hold values from 0 to 512, as said below
- active_count: int32 [8], P('region'), may hold values from 4 to 64, as said below
- conv_weight: bfloat16 [64, 64, 3, 3, 3], P('chan'), may hold values from -0.15625 to 0.15625
- down_weight: bfloat16 [128, 64, 2, 2, 2], P(None, 'chan'), may hold values from -0.25 to 0.25
Outputs:
- coarse: bfloat16 [512, 8192], P('region', 'chan')
Inputs may be any that keep to these rules, and one draw needn't show every extreme that they name: `destination`: each block of 16384 consecutive points names every region exactly 16384 / 8 times. Every point lies in an active brick of its region: voxel_slot // 512 < active_count[destination]. `adjacency`: entry n of row g names the brick at offset n from g, or 512 where that brick is inactive or off the map; rows of inactive slots hold only 512; the relation is symmetric. A neighbour at dx = 0 lies in g's own region, one at dx = -1 in that region or the previous one, one at dx = +1 in that region or the next one. In every region at most 16 active bricks have a neighbour in the next region and at most 16 in the previous one, and some region reaches 16 for each side. A region's active bricks fill its slots 0 to active_count - 1; some region fills all 64.
All inputs are finite; a program needn't handle non-finite values.
Results may differ from a plain program's by a relative error of at most 0.0053.
Values may be sent and summed in bfloat16 or wider, within the bound.
No kernel may reach another device: no remote copies, remote signals or barrier semaphores. Data moves between devices by JAX's collectives and lax.ppermute only.
A program may use at most 128 MiB of HBM per device.

v0:
```python
import jax
import jax.numpy as jnp
from jax import lax
from jax.sharding import PartitionSpec as P

OFFSETS = [
    (first, second, third)
    for first in (-1, 0, 1)
    for second in (-1, 0, 1)
    for third in (-1, 0, 1)
    if (first, second, third) != (0, 0, 0)
]
SOURCE = {-1: (7, 8), 0: (0, 8), 1: (0, 1)}
TARGET = {-1: (0, 1), 0: (1, 9), 1: (9, 10)}


def shifted(value, axis, steps):
    count = lax.axis_size(axis)
    first, last = (max(0, -steps), min(count, count - steps))
    return lax.ppermute(value, axis, [(source, source + steps) for source in range(first, last)])


def splat(columns, voxel_ids, slot_count):
    channels = columns.shape[0]
    totals = (
        jnp.zeros((channels, slot_count * 512), jnp.float32)
        .at[:, voxel_ids]
        .add(columns.astype(jnp.float32))
    )
    counts = jnp.zeros((slot_count * 512,), jnp.float32).at[voxel_ids].add(1.0)
    voxel_grid = (totals / jnp.maximum(counts, 1.0)).astype(jnp.bfloat16)
    return voxel_grid.reshape(channels, slot_count, 8, 8, 8).transpose(1, 0, 2, 3, 4)


def neighbour_planes(voxel_grid):
    slot_count = voxel_grid.shape[0]
    to_right = voxel_grid[:, :, 7]
    to_left = voxel_grid[:, :, 0]
    from_left = shifted(to_right, "region", 1)
    from_right = shifted(to_left, "region", -1)
    every_slot = jnp.arange(slot_count, dtype=jnp.int32)
    return (from_left, every_slot, from_right, every_slot)


def lookup(links, owners, region, slot_count, remote_ids, remote_owner):
    own_pos = links - region * slot_count
    remote_slot = links - remote_owner * slot_count
    matches = remote_slot[:, None] == remote_ids[None, :]
    remote_pos = jnp.argmax(matches, axis=1)
    capacity = remote_ids.shape[0]
    return jnp.where(
        owners == region,
        own_pos,
        jnp.where(owners == remote_owner, slot_count + remote_pos, slot_count + capacity),
    )


def body(point_feats, destination, voxel_slot, adjacency, active_count, conv_weight, down_weight):
    regions = lax.axis_size("region")
    region = lax.axis_index("region")
    slot_count = adjacency.shape[0]
    sorted_order = jnp.argsort(destination, stable=True)
    moved_feats, moved_ids = (
        lax.all_to_all(
            jnp.take(point_feats, sorted_order, axis=1),
            "region",
            split_axis=1,
            concat_axis=1,
            tiled=True,
        ),
        lax.all_to_all(
            jnp.take(voxel_slot, sorted_order)[None, :],
            "region",
            split_axis=1,
            concat_axis=1,
            tiled=True,
        ),
    )
    shard_grid = splat(moved_feats, moved_ids[0], slot_count)
    linked = adjacency < slot_count * regions
    owners = jnp.where(linked, adjacency // slot_count, regions + 7)
    full_grid = lax.all_gather(shard_grid, "chan", axis=1, tiled=True)
    left_planes, left_ids, right_planes, right_ids = neighbour_planes(full_grid)
    channel_total = full_grid.shape[1]
    zero_brick = jnp.zeros((1, channel_total, 8, 8, 8), jnp.bfloat16)
    zero_plane = zero_brick[:, :, 0]
    tables = {
        0: jnp.concatenate([full_grid, zero_brick], axis=0),
        -1: jnp.concatenate([full_grid[:, :, 7], left_planes, zero_plane], axis=0),
        1: jnp.concatenate([full_grid[:, :, 0], right_planes, zero_plane], axis=0),
    }
    local_pos = adjacency - region * slot_count
    positions = []
    slab_tables = []
    for number, offset in enumerate(OFFSETS):
        step_x, step_y, step_z = offset
        if step_x == 0:
            positions.append(
                jnp.where(owners[:, number] == region, local_pos[:, number], slot_count)
            )
            slab_tables.append(tables[0][:, :, :, slice(*SOURCE[step_y]), slice(*SOURCE[step_z])])
        else:
            remote_ids = left_ids if step_x == -1 else right_ids
            positions.append(
                lookup(
                    adjacency[:, number],
                    owners[:, number],
                    region,
                    slot_count,
                    remote_ids,
                    region + step_x,
                )
            )
            slab_tables.append(
                tables[step_x][:, :, None, slice(*SOURCE[step_y]), slice(*SOURCE[step_z])]
            )
    padded = jnp.pad(full_grid, ((0, 0), (0, 0), (1, 1), (1, 1), (1, 1)))
    for number, offset in enumerate(OFFSETS):
        picked = positions[number]
        slab = jnp.take(slab_tables[number], picked, axis=0)
        target = tuple((slice(*TARGET[element]) for element in offset))
        padded = padded.at[(slice(None), slice(None)) + target].set(slab)
    hidden = lax.conv_general_dilated(
        padded,
        conv_weight,
        (1, 1, 1),
        "VALID",
        dimension_numbers=("NCDHW", "OIDHW", "NCDHW"),
        preferred_element_type=jnp.float32,
    )
    alive_mask = (jnp.arange(slot_count, dtype=jnp.int32) < active_count[0]).astype(jnp.float32)[
        :, None, None, None, None
    ]
    hidden = (jnp.maximum(hidden, 0.0) * alive_mask).astype(jnp.bfloat16)
    partial_sums = lax.conv_general_dilated(
        hidden,
        down_weight,
        (2, 2, 2),
        "VALID",
        dimension_numbers=("NCDHW", "OIDHW", "NCDHW"),
        preferred_element_type=jnp.float32,
    )
    summed = lax.psum_scatter(partial_sums, "chan", scatter_dimension=1, tiled=True)
    return jnp.maximum(summed, 0.0).astype(jnp.bfloat16).reshape(slot_count, -1)


def solution(mesh):
    return jax.shard_map(
        body,
        mesh=mesh,
        in_specs=(
            P("chan", "region"),
            P("region"),
            P("region"),
            P("region", None),
            P("region"),
            P("chan", None, None, None, None),
            P(None, "chan", None, None, None),
        ),
        out_specs=P("region", "chan"),
        check_vma=False,
    )
```

profile of v0, /device:TPU:0, one launch (start us, length us, event | category | flops | bytes accessed | tf_op | source)
XLA Modules:
  0.0 952.2 jit_solution(711282797337326921)
XLA Ops:
  6.5 8.6 sort.17
  15.3 90.5 %gather_fusion = s32[16384]{0:T(1024)S(1)} fusion(s32[16384]{0:T(1024)S(1)} %copy-done.1, s32[16384]{0:T(1024)S(1)} %fusion.21), kind=kCustom, calls=%fused_computation.26 | custom fusion | bytes 196608 | tf_op jit(solution)/shard_map/jit(_take)/gather | solution.py:72
  106.4 7.3 all-to-all-start
  117.6 3.1 copy.166
  120.7 57.7 %gather_fusion.1 = bf16[16384,16]{1,0:T(8,128)(2,1)} fusion(bf16[16,16384]{0,1:T(8,128)(2,1)} %copy.166, s32[16384]{0:T(1024)S(1)} %fusion.21), kind=kCustom, calls=%fused_computation.27 | custom fusion | bytes 1114112 | tf_op jit(solution)/shard_map/jit(_take)/gather | solution.py:65
  178.4 3.5 copy.167
  183.5 6.0 all-to-all-start.1
  189.7 86.1 %scatter_custom_fusion.1 = f32[32768]{0:T(1024)S(1)} fusion(s32[16384]{0:T(1024)S(1)} %bitcast.474, f32[16384]{0:T(1024)S(1)} %broadcast.623, f32[]{:T(128)} %constant.1017.clone.1), kind=kCustom, calls=%fused_computation.89 | custom fusion | flops 16384 | bytes 131076 | tf_op jit(solution)/shard_map/scatter-add | solution.py:30
  275.9 4.6 copy.169
  280.6 94.4 %scatter_custom_fusion = f32[16,32768]{0,1:T(8,128)} fusion(s32[16384]{0:T(1024)S(1)} %bitcast.475, f32[16384,16]{1,0:T(8,128)} %copy.169, f32[]{:T(128)} %constant.1017.clone.1), kind=kCustom, calls=%fused_computation.33 | custom fusion | flops 262144 | bytes 2097664 | tf_op jit(solution)/shard_map/scatter-add | solution.py:28
  374.9 16.8 %divide_convert_fusion = bf16[16,32768]{0,1:T(8,128)(2,1)} fusion(f32[16,32768]{0,1:T(8,128)} %scatter_custom_fusion, f32[32768]{0:T(1024)S(1)} %broadcast_maximum_fusion), kind=kLoop, calls=%fused_computation.30 | loop fusion | flops 1048576 | bytes 3276800 | tf_op jit(solution)/shard_map/convert_element_type | solution.py:31
  391.7 13.0 %copy.170 = bf16[16,64,8,8,8]{1,4,3,2,0:T(8,128)(2,1)} copy(bf16[16,64,8,8,8]{0,4,3,2,1:T(8,128)(2,1)} %bitcast.468) | data formatting | bytes 2097152 | tf_op jit(solution)/shard_map/reshape | solution.py:32
  424.0 41.4 %all-gather.2.cloned.1.call-done = bf16[64,64,8,8,8]{0,4,3,2,1:T(8,128)(2,1)} async-done(((bf16[64,16,8,8,8]{0,4,3,2,1:T(8,128)(2,1)}), bf16[64,64,8,8,8]{0,4,3,2,1:T(8,128)(2,1)}) %all-gather.2.cloned.1.call-update) | async-done | bytes 4194320 | tf_op jit(solution)/shard_map/all_gather | solution.py:82
  465.4 14.5 %copy.186 = bf16[64,64,8,8,8]{1,2,0,4,3:T(8,128)(2,1)} copy(bf16[64,64,8,8,8]{0,4,3,2,1:T(8,128)(2,1)} %all-gather.2.cloned.1.call-done) | data formatting | bytes 8388608 | tf_op jit(solution)/shard_map/all_gather | solution.py:82
  481.3 2.3 copy-done.2
  483.5 1.8 fusion.14
  486.7 2.7 fusion.35
  489.4 2.9 copy.219
  492.4 2.0 copy.218
  494.4 4.4 collective-permute-start
  507.1 1.5 copy.196
  508.6 2.5 copy.188
  511.9 2.0 gather_fusion.12
  513.9 1.6 bitcast_select_fusion.1
  515.5 4.1 copy.197
  519.6 4.0 copy.189
  527.9 6.5 copy.194
  534.4 4.3 copy.192
  538.8 11.3 %pad.109 = bf16[64,64,10,10,10]{0,4,3,2,1:T(8,128)(2,1)} pad(bf16[64,64,8,8,8]{0,4,3,2,1:T(8,128)(2,1)} %all-gather.2.cloned.1.call-done, bf16[]{:T(256)} %constant.1025.clone.1), padding=0_0x0_0x1_1x1_1x1_1 | pad | bytes 12386306 | tf_op jit(solution)/shard_map/jit(_pad)/pad | solution.py:117
  550.1 2.8 maximum_maximum_fusion.1
  554.8 1.9 copy.178
  581.0 2.3 gather_fusion.6
  583.4 1.7 bitcast_select_fusion.5
  585.1 4.0 copy.179
  590.9 3.1 copy.207
  604.3 1.7 scatter.86
  606.0 1.9 scatter.89
  607.9 1.7 scatter.90
  609.6 7.7 scatter.91
  617.3 14.7 %scatter.94 = bf16[64,64,10,10,10]{0,4,3,2,1:T(8,128)(2,1)} dynamic-update-slice(bf16[64,64,10,10,10]{0,4,3,2,1:T(8,128)(2,1)} %scatter.91, bf16[64,64,1,8,8]{0,4,3,2,1:T(8,128)(2,1)} %copy.179, s32[]{:T(128)} %constant.1018.clone.1, s32[]{:T(128)} %constant.1018.clone.1, s32[]{:T(128)} %constant.1018.clone.1, s32[]{:T(128)} %constant.1027.clone.1, s32[]{:T(128)} %constant.1027.clone.1) | dynamic-update-slice | bytes 1048580 | tf_op jit(solution)/shard_map/scatter | solution.py:122
  632.0 7.7 scatter.95
  639.6 1.7 scatter.96
  641.3 1.9 scatter.99
  643.2 1.7 scatter.100
  644.8 7.7 scatter.101
  652.6 14.8 %scatter.104 = bf16[64,64,10,10,10]{0,4,3,2,1:T(8,128)(2,1)} dynamic-update-slice(bf16[64,64,10,10,10]{0,4,3,2,1:T(8,128)(2,1)} %scatter.101, bf16[64,64,8,1,8]{0,4,3,2,1:T(8,128)(2,1)} %copy.189, s32[]{:T(128)} %constant.1018.clone.1, s32[]{:T(128)} %constant.1018.clone.1, s32[]{:T(128)} %constant.1027.clone.1, s32[]{:T(128)} %constant.1018.clone.1, s32[]{:T(128)} %constant.1027.clone.1) | dynamic-update-slice | bytes 1048580 | tf_op jit(solution)/shard_map/scatter | solution.py:122
  667.3 7.8 scatter.105
  675.1 52.5 %scatter.106 = bf16[64,64,10,10,10]{0,4,3,2,1:T(8,128)(2,1)} dynamic-update-slice(bf16[64,64,10,10,10]{0,4,3,2,1:T(8,128)(2,1)} %scatter.105, bf16[64,64,8,8,1]{0,4,3,2,1:T(2,128)(2,1)} %copy.192, s32[]{:T(128)} %constant.1018.clone.1, s32[]{:T(128)} %constant.1018.clone.1, s32[]{:T(128)} %constant.1027.clone.1, s32[]{:T(128)} %constant.1027.clone.1, s32[]{:T(128)} %constant.1018.clone.1) | dynamic-update-slice | bytes 1048580 | tf_op jit(solution)/shard_map/scatter | solution.py:122
  727.6 52.4 %scatter.109 = bf16[64,64,10,10,10]{0,4,3,2,1:T(8,128)(2,1)} dynamic-update-slice(bf16[64,64,10,10,10]{0,4,3,2,1:T(8,128)(2,1)} %scatter.106, bf16[64,64,8,8,1]{0,4,3,2,1:T(2,128)(2,1)S(1)} %copy-done.3, s32[]{:T(128)} %constant.1018.clone.1, s32[]{:T(128)} %constant.1018.clone.1, s32[]{:T(128)} %constant.1027.clone.1, s32[]{:T(128)} %constant.1027.clone.1, s32[]{:T(128)} %constant.1037.clone.1) | dynamic-update-slice | bytes 1048580 | tf_op jit(solution)/shard_map/scatter | solution.py:122
  780.0 7.7 scatter.110
  787.7 14.1 %scatter.111 = bf16[64,64,10,10,10]{0,4,3,2,1:T(8,128)(2,1)} dynamic-update-slice(bf16[64,64,10,10,10]{0,4,3,2,1:T(8,128)(2,1)} %scatter.110, bf16[64,64,8,1,8]{0,4,3,2,1:T(8,128)(2,1)S(1)} %copy-done.4, s32[]{:T(128)} %constant.1018.clone.1, s32[]{:T(128)} %constant.1018.clone.1, s32[]{:T(128)} %constant.1027.clone.1, s32[]{:T(128)} %constant.1037.clone.1, s32[]{:T(128)} %constant.1027.clone.1) | dynamic-update-slice | bytes 1048580 | tf_op jit(solution)/shard_map/scatter | solution.py:122
  801.8 7.7 scatter.114
  809.5 1.7 scatter.115
  811.2 1.8 scatter.116
  812.9 1.7 scatter.119
  814.6 7.7 scatter.120
  822.3 14.6 %scatter.121 = bf16[64,64,10,10,10]{0,4,3,2,1:T(8,128)(2,1)} dynamic-update-slice(bf16[64,64,10,10,10]{0,4,3,2,1:T(8,128)(2,1)} %scatter.120, bf16[64,64,1,8,8]{0,4,3,2,1:T(8,128)(2,1)} %copy.207, s32[]{:T(128)} %constant.1018.clone.1, s32[]{:T(128)} %constant.1018.clone.1, s32[]{:T(128)} %constant.1037.clone.1, s32[]{:T(128)} %constant.1027.clone.1, s32[]{:T(128)} %constant.1027.clone.1) | dynamic-update-slice | bytes 1048580 | tf_op jit(solution)/shard_map/scatter | solution.py:122
  836.9 7.7 scatter.124
  844.6 1.7 scatter.125
  846.3 1.8 scatter.126
  848.0 1.7 scatter.129
  849.8 44.1 %multiply_convert_fusion.clone.4 = bf16[64,16,8,8,8]{0,1,4,3,2:T(8,128)(2,1)S(1)} fusion(bf16[16,64,3,3,3]{1,0,4,3,2:T(8,128)(2,1)S(1)} %copy-done, bf16[64,64,10,10,10]{0,4,3,2,1:T(8,128)(2,1)} %scatter.129, f32[64]{0:T(128)S(1)} %copy-done.23), kind=kOutput, calls=%fused_computation.35.clone.clone.clone.1 | convolution fusion | flops 1813512192 | bytes 9296128 | tf_op jit(solution)/shard_map/conv_general_dilated | solution.py:123
  893.9 2.7 fusion.7
  896.6 45.8 %reduce-scatter.2.cloned.1.call-done = f32[64,32,4,4,4]{0,1,4,3,2:T(8,128)} async-done(((f32[64,128,4,4,4]{0,1,4,3,2:T(8,128)}), f32[64,32,4,4,4]{0,1,4,3,2:T(8,128)}) %reduce-scatter.2.cloned.1.call-update) | async-done | bytes 524304 | tf_op jit(solution)/shard_map/reduce_scatter | solution.py:143
  (196 shorter events, 81.9 us)
Async XLA Ops:
  6.5 843.2 %copy-start = (bf16[16,64,3,3,3]{1,0,4,3,2:T(8,128)(2,1)S(1)}, bf16[16,64,3,3,3]{1,0,4,3,2:T(8,128)(2,1)}, u32[]{:S(2)}) copy-start(bf16[16,64,3,3,3]{1,0,4,3,2:T(8,128)(2,1)} %param.78) | copy-start | bytes 165892
  6.5 8.7 copy-start.1
  15.2 99.1 %copy-start.10 = (s32[64,26]{0,1:T(8,128)S(1)}, s32[64,26]{0,1:T(8,128)}, u32[]{:S(2)}) copy-start(s32[64,26]{0,1:T(8,128)} %param.76) | copy-start | bytes 19972
  15.2 102.3 %copy-start.6 = (bf16[16,16384]{1,0:T(8,128)(2,1)S(1)}, bf16[16,16384]{1,0:T(8,128)(2,1)}, u32[]{:S(2)}) copy-start(bf16[16,16384]{1,0:T(8,128)(2,1)} %param.73) | copy-start | bytes 1572868
  106.4 77.1 %all-to-all-start = ((s32[1,8,2048]{2,0,1:T(1,128)}), s32[1,8,2048]{2,0,1:T(1,128)S(1)}, u32[]{:S(2)}, u32[]{:S(2)}) async-start(s32[1,8,2048]{2,0,1:T(1,128)} %bitcast), calls=%async_computation | async-start | bytes 131072 | tf_op jit(solution)/shard_map/all_to_all | solution.py:71
  183.5 92.2 %all-to-all-start.1 = ((bf16[16,8,2048]{2,0,1:T(8,128)(2,1)}), bf16[16,8,2048]{2,0,1:T(8,128)(2,1)S(1)}, u32[]{:S(2)}, u32[]{:S(2)}) async-start(bf16[16,8,2048]{2,0,1:T(8,128)(2,1)} %broadcast_select_fusion), calls=%async_computation.1 | async-start | bytes 1048576 | tf_op jit(solution)/shard_map/all_to_all | solution.py:64
  189.5 275.9 %all-gather.2.cloned.1.call-start = ((), (), s32[]{:S(2)}) async-start(), calls=%async_computation.3 | async-start | bytes 10485760 | tf_op jit(solution)/shard_map/all_gather | solution.py:82
  404.7 537.7 %reduce-scatter.2.cloned.1.call-start = ((), (), s32[]{:S(2)}) async-start(), calls=%async_computation.4 | async-start | bytes 5242880 | tf_op jit(solution)/shard_map/reduce_scatter | solution.py:143
  479.9 3.6 copy-start.2
  494.4 55.7 %collective-permute-start = (bf16[64,64,8,8]{1,0,3,2:T(8,128)(2,1)}, bf16[64,64,8,8]{1,0,3,2:T(8,128)(2,1)}, u32[]{:S(2)}, u32[]{:S(2)}) collective-permute-start(bf16[64,64,8,8]{1,0,3,2:T(8,128)(2,1)} %bitcast.12), channel_id=1, source_target_pairs={{0,4},{4,8},{8,12},{12,16},{16,20},{20,24},{24,28},{1,5},{5,9},{9,... | collective-permute-start | bytes 1572872 | tf_op jit(solution)/shard_map/ppermute | solution.py:20
  498.7 51.3 %collective-permute-start.1 = (bf16[64,64,8,8]{1,0,3,2:T(8,128)(2,1)}, bf16[64,64,8,8]{1,0,3,2:T(8,128)(2,1)}, u32[]{:S(2)}, u32[]{:S(2)}) collective-permute-start(bf16[64,64,8,8]{1,0,3,2:T(8,128)(2,1)} %bitcast.99), channel_id=1, source_target_pairs={{4,0},{8,4},{12,8},{16,12},{20,16},{24,20},{28,24},{5,1},{9,5},{13... | collective-permute-start | bytes 1572872 | tf_op jit(solution)/shard_map/ppermute | solution.py:20
  552.9 5.2 copy-start.18
  552.9 6.7 copy-start.17
  552.9 8.2 copy-start.19
  552.9 9.8 %copy-start.22 = (pred[64]{0:T(512)(128)(4,1)S(1)}, pred[64]{0:T(512)(128)(4,1)}, u32[]{:S(2)}) copy-start(pred[64]{0:T(512)(128)(4,1)} %get-tuple-element.458) | copy-start | bytes 196
  552.9 11.3 %copy-start.13 = (pred[64]{0:T(512)(128)(4,1)S(1)}, pred[64]{0:T(512)(128)(4,1)}, u32[]{:S(2)}) copy-start(pred[64]{0:T(512)(128)(4,1)} %get-tuple-element.468) | copy-start | bytes 196
  552.9 12.8 %copy-start.21 = (pred[64]{0:T(512)(128)(4,1)S(1)}, pred[64]{0:T(512)(128)(4,1)}, u32[]{:S(2)}) copy-start(pred[64]{0:T(512)(128)(4,1)} %get-tuple-element.462) | copy-start | bytes 196
  552.9 14.4 %copy-start.20 = (pred[64]{0:T(512)(128)(4,1)S(1)}, pred[64]{0:T(512)(128)(4,1)}, u32[]{:S(2)}) copy-start(pred[64]{0:T(512)(128)(4,1)} %get-tuple-element.366) | copy-start | bytes 196
  552.9 15.9 %copy-start.16 = (pred[64]{0:T(512)(128)(4,1)S(1)}, pred[64]{0:T(512)(128)(4,1)}, u32[]{:S(2)}) copy-start(pred[64]{0:T(512)(128)(4,1)} %get-tuple-element.362) | copy-start | bytes 196
  589.1 6.7 copy-start.12
  590.1 8.5 copy-start.15
  590.1 9.6 %copy-start.5 = (bf16[129,64,8]{1,0,2:T(8,128)(2,1)S(1)}, bf16[129,64,8]{1,0,2:T(8,128)(2,1)}, u32[]{:S(2)}) copy-start(bf16[129,64,8]{1,0,2:T(8,128)(2,1)} %get-tuple-element.507) | copy-start | bytes 396292
  590.1 10.6 %copy-start.14 = (pred[64]{0:T(512)(128)(4,1)S(1)}, pred[64]{0:T(512)(128)(4,1)}, u32[]{:S(2)}) copy-start(pred[64]{0:T(512)(128)(4,1)} %get-tuple-element.446) | copy-start | bytes 196
  599.7 127.9 %copy-start.3 = (bf16[64,64,8,8,1]{0,4,3,2,1:T(2,128)(2,1)S(1)}, bf16[64,64,8,8,1]{0,4,3,2,1:T(2,128)(2,1)}, u32[]{:S(2)}) copy-start(bf16[64,64,8,8,1]{0,4,3,2,1:T(2,128)(2,1)} %copy.194) | copy-start | bytes 1572868
  602.5 185.1 %copy-start.4 = (bf16[64,64,8,1,8]{0,4,3,2,1:T(8,128)(2,1)S(1)}, bf16[64,64,8,1,8]{0,4,3,2,1:T(8,128)(2,1)}, u32[]{:S(2)}) copy-start(bf16[64,64,8,1,8]{0,4,3,2,1:T(8,128)(2,1)} %copy.197) | copy-start | bytes 1572868
  617.3 193.9 %copy-start.8 = (bf16[64,64,1,1,8]{0,4,3,2,1:T(8,128)(2,1)S(1)}, bf16[64,64,1,1,8]{0,4,3,2,1:T(8,128)(2,1)}, u32[]{:S(2)}) copy-start(bf16[64,64,1,1,8]{0,4,3,2,1:T(8,128)(2,1)} %copy.202) | copy-start | bytes 196612
  652.6 192.0 %copy-start.9 = (bf16[64,64,1,1,1]{0,4,3,2,1:T(2,128)(2,1)S(1)}, bf16[64,64,1,1,1]{0,4,3,2,1:T(2,128)(2,1)}, u32[]{:S(2)}) copy-start(bf16[64,64,1,1,1]{0,4,3,2,1:T(2,128)(2,1)} %copy.210) | copy-start | bytes 24580
  652.6 193.7 %copy-start.7 = (bf16[64,64,1,1,8]{0,4,3,2,1:T(8,128)(2,1)S(1)}, bf16[64,64,1,1,8]{0,4,3,2,1:T(8,128)(2,1)}, u32[]{:S(2)}) copy-start(bf16[64,64,1,1,8]{0,4,3,2,1:T(8,128)(2,1)} %copy.212) | copy-start | bytes 196612
  667.3 182.4 %copy-start.23 = (f32[64]{0:T(128)S(1)}, f32[64]{0:T(128)}, u32[]{:S(2)}) copy-start(f32[64]{0:T(128)} %compare_convert_fusion) | copy-start | bytes 772
  849.7 44.1 %copy-start.11 = (bf16[128,16,2,2,2]{0,4,3,2,1:T(2,128)(2,1)S(1)}, bf16[128,16,2,2,2]{0,4,3,2,1:T(2,128)(2,1)}, u32[]{:S(2)}) copy-start(bf16[128,16,2,2,2]{0,4,3,2,1:T(2,128)(2,1)} %param.79) | copy-start | bytes 98308
Sparse Core Ops, SparseCore 0:
  404.8 60.5 all-gather.1
  896.7 45.6 reduce-scatter.1
where the time goes:
time: 966 us; the launch traced here: 952 us
  local copies, waits for them, and re-layouts  539 us (56%)
  other arithmetic  245 us (25%)
  waiting for transfers between devices  87.2 us (9%)
  matrix products  46.8 us (5%)
  starting transfers between devices  19.4 us (2%)
  between operations  15.1 us (2%)
    scatter x26, local copies, waits for them, and re-layouts, body(): padded = padded.at[(slice(None), slice(None)) + target].set(slab)  245 us
    scatter-add x1, other arithmetic, splat(): totals = jnp.zeros((channels, slot_count * 512), jnp.float32).at[:, voxel...  94.4 us
    gather x1, local copies, waits for them, and re-layouts, body(): jnp.take(voxel_slot, sorted_order)[None, :]  90.5 us
    scatter-add x1, other arithmetic, splat(): counts = jnp.zeros((slot_count * 512,), jnp.float32).at[voxel_ids].add(1.0)  86.1 us
    gather x2, local copies, waits for them, and re-layouts, body(): jnp.take(point_feats, sorted_order, axis=1)  61.2 us
    reduce_scatter x1, waiting for transfers between devices, body(): lax.psum_scatter(partial_sums, 'chan', scatter_dimension=1, tiled=True)  45.8 us
    conv_general_dilated x1, matrix products, body(): lax.conv_general_dilated(padded, conv_weight, (1, 1, 1), 'VALID', dimensi...  44.1 us
    select_n x26, local copies, waits for them, and re-layouts, body(): slab = jnp.take(slab_tables[number], picked, axis=0)  42.6 us
  transfers between devices with their start and end apart: 6, of which 2 were waited for; matrix products, arithmetic and copies ran while one was open for 24% of the time, Pallas kernels for 0%

commit v1 on v0

v1 whole, which is shorter than its diff:
```python
import functools

import jax
import jax.numpy as jnp
import numpy as np
from jax import lax
from jax.experimental import pallas as pl
from jax.experimental.pallas import tpu as pltpu
from jax.sharding import PartitionSpec as P

OFFSETS = [
    (first, second, third)
    for first in (-1, 0, 1)
    for second in (-1, 0, 1)
    for third in (-1, 0, 1)
    if (first, second, third) != (0, 0, 0)
]
LANES = 128
REACH = 16
F32 = jnp.float32
BF16 = jnp.bfloat16
NT = (((1,), (1,)), ((), ()))
VMEM = pl.BlockSpec(memory_space=pltpu.VMEM)
SMEM = pl.BlockSpec(memory_space=pltpu.SMEM)


def mm(a, b):
    return jnp.dot(a, b, preferred_element_type=F32)


def params():
    return pltpu.CompilerParams(vmem_limit_bytes=48 * 1024 * 1024)


def permute_kernel(depth, feats, order, out, stack):
    channels, points = feats.shape
    high = points // depth
    for part in range(high):
        stack[part * channels : (part + 1) * channels, :] = feats[:, part * depth : (part + 1) * depth]
    blocks = out.shape[1]
    pairs = order.shape[0] // 2

    def step(at, _):
        wanted = order[pl.ds(at * 2, 2), :]
        wanted = jnp.concatenate([wanted[0:1], wanted[1:2]], axis=1)
        low = wanted & (depth - 1)
        top = wanted // depth
        hot = (lax.broadcasted_iota(jnp.int32, (depth, 2 * LANES), 0) == low).astype(BF16)
        found = mm(stack[...], hot)
        picked = jnp.zeros((channels, 2 * LANES), F32)
        for part in range(high):
            picked = jnp.where(top == part, found[part * channels : (part + 1) * channels], picked)
        picked = picked.astype(BF16)
        for half in range(2):
            tile = at * 2 + half
            out[tile // blocks, tile % blocks] = picked[:, half * LANES : (half + 1) * LANES]
        return 0

    lax.fori_loop(0, pairs, step, 0)


def permute(feats, order, regions):
    channels, points = feats.shape
    depth = 512
    return pl.pallas_call(
        functools.partial(permute_kernel, depth),
        out_shape=jax.ShapeDtypeStruct((regions, points // regions // LANES, channels, LANES), BF16),
        in_specs=[VMEM, VMEM],
        out_specs=VMEM,
        scratch_shapes=[pltpu.VMEM((points // depth * channels, depth), BF16)],
        compiler_params=params(),
        name="permute",
    )(feats, order)


WINDOW = 256
GROUP = 8


def voxel_kernel(slots, feats, ids, first, last, hops, send_pos, out, faces, acc):
    chunks, blocks, channels, _ = feats.shape
    groups = chunks // GROUP
    windows = slots * 64 // WINDOW
    per_plane = slots * 8 // WINDOW
    devices = out.shape[0]

    def window(number):
        acc[...] = jnp.zeros_like(acc)

        def one_group(group, _):
            def step(at, _):
                sides = []
                rows = []
                for member in range(GROUP):
                    chunk = group * GROUP + member
                    block = first[number, chunk] + at
                    valid = block < last[number, chunk]
                    block = jnp.minimum(block, blocks - 1)
                    code = ids[chunk, pl.ds(block, 1), :]
                    cell = code & 7
                    rows.append(jnp.where(valid, code >> 3, -1))
                    values = feats[chunk, block].astype(F32)
                    mask = [cell == k for k in range(8)]
                    side = [jnp.where(m, values, 0.0).astype(BF16) for m in mask]
                    side += [jnp.broadcast_to(jnp.where(m, 1.0, 0.0), (channels, LANES)).astype(BF16) for m in mask]
                    sides.append(jnp.concatenate(side, axis=0))
                side = jnp.concatenate(sides, axis=1)
                row = jnp.concatenate(rows, axis=1)
                hot = lax.broadcasted_iota(jnp.int32, (WINDOW, GROUP * LANES), 0) + number * WINDOW == row
                acc[...] += lax.dot_general(hot.astype(BF16), side, NT, preferred_element_type=F32)
                return 0

            lax.fori_loop(0, hops[number, group], step, 0)
            return 0

        if groups == 1:
            one_group(0, 0)
        else:
            lax.fori_loop(0, groups, one_group, 0)
        mean = (acc[:, :LANES] / jnp.maximum(acc[:, LANES:], 1.0)).astype(BF16)
        plane = number // per_plane
        begin = (number % per_plane) * WINDOW
        owner = plane // 2
        out[owner, 1 + plane % 2, begin : begin + WINDOW, :] = mean
        if plane % 2 == 0:
            out[(owner - 1) % devices, 3, begin : begin + WINDOW, :] = mean
        else:
            out[(owner + 1) % devices, 0, begin : begin + WINDOW, :] = mean

    for number in range(windows):
        window(number)
    for side in range(2):
        hot = lax.broadcasted_iota(jnp.int32, (REACH, slots), 0) == send_pos[side : side + 1, :]
        hot = jnp.where(hot, 1.0, 0.0).astype(BF16)
        for j in range(8):
            if side == 0:
                plane = out[devices - 1, 2, j * slots : (j + 1) * slots, :]
            else:
                plane = out[0, 1, j * slots : (j + 1) * slots, :]
            faces[side, j] = mm(hot, plane).astype(BF16)


def voxels(feats, ids, send_pos, slots, devices):
    chunks, blocks, channels, _ = feats.shape
    windows = slots * 64 // WINDOW
    bounds = (jnp.arange(windows + 1, dtype=jnp.int32) * (WINDOW * 8))[:, None, None, None]
    before = jnp.sum((ids[None] < bounds).astype(jnp.int32), axis=(2, 3))
    first = before[:-1] // LANES
    last = (before[1:] + LANES - 1) // LANES
    hops = jnp.max((last - first).reshape(windows, chunks // GROUP, GROUP), axis=2)
    return pl.pallas_call(
        functools.partial(voxel_kernel, slots),
        out_shape=(
            jax.ShapeDtypeStruct((devices, 4, 8 * slots, LANES), BF16),
            jax.ShapeDtypeStruct((2, 8, REACH, LANES), BF16),
        ),
        in_specs=[VMEM, VMEM, SMEM, SMEM, SMEM, VMEM],
        out_specs=(VMEM, VMEM),
        scratch_shapes=[pltpu.VMEM((WINDOW, 2 * LANES), F32)],
        compiler_params=params(),
        name="voxels",
    )(feats, ids, first, last, hops, send_pos)


def spread_matrix():
    spread = np.zeros((4, 384, 192), np.float32)
    for k in range(4):
        for e in range(3):
            cell = k + e
            for channel in range(64):
                source, inner = divmod(channel, 16)
                if 1 <= cell <= 4:
                    row = source * 64 + (cell - 1) * 16 + inner
                else:
                    row = 256 + (cell // 5) * 64 + source * 16 + inner
                spread[k, row, e * 64 + channel] = 1
    return spread


def weight_kernel(spread, weights, out):
    for ab in range(9):
        for k in range(4):
            out[ab, :, k * 64 : (k + 1) * 64] = lax.dot_general(
                spread[k], weights[ab], NT, preferred_element_type=F32
            ).astype(BF16)


def banded(weights):
    return pl.pallas_call(
        weight_kernel,
        out_shape=jax.ShapeDtypeStruct((9, 384, 256), BF16),
        in_specs=[VMEM, VMEM],
        out_specs=VMEM,
        compiler_params=params(),
        name="banded",
    )(jnp.asarray(spread_matrix(), BF16), weights)


def halo_matrix():
    pick = np.zeros((512, 256), np.float32)
    for group, cell in enumerate((7, 0, 3, 4)):
        for source in range(4):
            for inner in range(16):
                pick[source * 128 + cell * 16 + inner, group * 64 + source * 16 + inner] = 1
    return pick


def conv_kernel(slots, active, grid, remote, hot, pick, weights, down, out, table, padded, stacked):
    rows = slots * 8
    extra = REACH
    total = slots + extra
    low = lax.broadcasted_iota(jnp.int32, (slots, LANES), 1) < 64

    def arrange(parts, plane, j, at, count):
        for half in range(2):
            cut = slice(half * 64, half * 64 + 64)
            for pair in range(2):
                both = jnp.concatenate([parts[2 * pair][:, cut], parts[2 * pair + 1][:, cut]], axis=1)
                table[plane, j, at : at + count, half * 384 + pair * 128 : half * 384 + pair * 128 + 128] = both

    for plane in range(4):
        whole = jnp.concatenate([grid[source, plane] for source in range(4)], axis=1)
        edge = mm(whole, pick[...]).astype(BF16)
        for j in range(8):
            arrange([grid[s, plane, j * slots : (j + 1) * slots, :] for s in range(4)], plane, j, 0, slots)
            table[plane, j, 0:slots, 256:384] = edge[j * slots : (j + 1) * slots, :128]
            table[plane, j, 0:slots, 640:768] = edge[j * slots : (j + 1) * slots, 128:]
    for plane in (0, 3):
        for j in range(8):
            parts = [remote[s, j] for s in range(4)]
            arrange(parts, plane, j, slots, extra)
            edge = mm(jnp.concatenate(parts, axis=1), pick[...]).astype(BF16)
            table[plane, j, slots:total, 256:384] = edge[:, :128]
            table[plane, j, slots:total, 640:768] = edge[:, 128:]

    for plane in range(4):
        base = (0, 9, 9, 18)[plane]
        used = total if plane in (0, 3) else slots
        for jj in range(10):
            dy, j = ((-1, 7) if jj == 0 else (1, 0) if jj == 9 else (0, jj - 1))
            at = base + (dy + 1) * 3
            source = table[plane, j, 0:used, :]
            if plane in (1, 2) and dy == 0:
                own = source
            else:
                own = mm(hot[at + 1, :, 0:used], source).astype(BF16)
            near = source[:, 256:384]
            down_edge = mm(hot[at, :, 0:used], near).astype(BF16)
            up_edge = mm(hot[at + 2, :, 0:used], near).astype(BF16)
            kept = own[:, 640:768]
            padded[plane, jj, :, 0:256] = own[:, 0:256]
            padded[plane, jj, :, 256:384] = jnp.where(low, down_edge, kept)
            padded[plane, jj, :, 384:640] = own[:, 384:640]
            padded[plane, jj, :, 640:768] = jnp.where(low, kept, up_edge)

    alive = lax.broadcasted_iota(jnp.int32, (slots, 256), 0) < active[0]
    for half in range(2):
        for a_out in range(2):
            total_sum = jnp.zeros((rows, 256), F32)
            for a in range(3):
                for b in range(3):
                    left = padded[a_out + a, b : b + 8, :, half * 384 : half * 384 + 384].reshape(rows, 384)
                    total_sum += mm(left, weights[a * 3 + b])
            for j in range(8):
                block = jnp.where(alive, jnp.maximum(total_sum[j * slots : (j + 1) * slots], 0.0), 0.0).astype(BF16)
                for kk in range(2):
                    begin = ((j // 2) * 4 + half * 2 + kk) * slots
                    place = (a_out * 2 + j % 2) * 128
                    stacked[begin : begin + slots, place : place + 128] = block[:, kk * 128 : kk * 128 + 128]

    result = lax.dot_general(down[...], stacked[...], NT, preferred_element_type=F32)
    result = jnp.maximum(result, 0.0).astype(BF16)
    devices = out.shape[0]
    width = out.shape[1]
    for device in range(devices):
        out[device] = result[device * width : (device + 1) * width]


def convolve(active, grid, remote, hot, weights, down):
    devices = grid.shape[0]
    slots = grid.shape[2] // 8
    outputs = down.shape[0]
    return pl.pallas_call(
        functools.partial(conv_kernel, slots),
        out_shape=jax.ShapeDtypeStruct((devices, outputs // devices, 16 * slots), BF16),
        in_specs=[SMEM] + [VMEM] * 6,
        out_specs=VMEM,
        scratch_shapes=[
            pltpu.VMEM((4, 8, slots + REACH, 768), BF16),
            pltpu.VMEM((4, 10, slots, 768), BF16),
            pltpu.VMEM((16 * slots, 512), BF16),
        ],
        compiler_params=params(),
        name="convolve",
    )(active, grid, remote, hot, jnp.asarray(halo_matrix(), BF16), weights, down)


def final_kernel(slots, data, out, turned):
    planes, outputs, _ = data.shape
    for plane in range(planes):
        for cell in range(16):
            turned[pl.ds(plane * 16 + cell, outputs, stride=64), :] = data[
                plane, :, cell * slots : (cell + 1) * slots
            ].astype(F32)
    for tile in range(out.shape[1] // LANES):
        out[:, tile * LANES : (tile + 1) * LANES] = turned[tile * LANES : (tile + 1) * LANES, :].T.astype(BF16)


def finish(data, slots):
    outputs = data.shape[1]
    return pl.pallas_call(
        functools.partial(final_kernel, slots),
        out_shape=jax.ShapeDtypeStruct((slots, outputs * 64), BF16),
        in_specs=[VMEM],
        out_specs=VMEM,
        scratch_shapes=[pltpu.VMEM((outputs * 64, slots), F32)],
        compiler_params=params(),
        name="finish",
    )(data)


def links(adjacency, region, regions, chan, devices):
    slots = adjacency.shape[0]
    named = adjacency.T
    linked = named < slots * regions
    owner = jnp.where(linked, named // slots, regions + 7)
    slot = named % slots
    every = jnp.arange(slots, dtype=jnp.int32)
    steps = np.array([offset[0] for offset in OFFSETS])
    send_pos = []
    place = {}
    for step in (1, -1):
        rows = np.nonzero(steps == step)[0]
        owns = owner[rows[0] : rows[-1] + 1] == region + step
        sends = jnp.any(owns, axis=0)
        rank = jnp.sum((sends[None, :] & (every[None, :] < every[:, None])).astype(jnp.int32), axis=1)
        send_pos.append(jnp.where(sends, rank, -1))
        there = slot[rows[0] : rows[-1] + 1]
        member = jnp.any(owns[:, :, None] & (there[:, :, None] == every), axis=(0, 1))
        below = jnp.sum(
            (member[None, None, :] & (every < there[:, :, None])).astype(jnp.int32), axis=2
        )
        place[step] = jnp.where(owns, slots + below, -1)
    own = jnp.where(owner == region, slot, -1)
    same = jnp.concatenate([own[9:13], every[None, :], own[13:17]], axis=0)
    left = jnp.where(owner[0:9] == region, slot[0:9], place[-1])
    right = jnp.where(owner[17:26] == region, slot[17:26], place[1])
    first = jnp.where(chan == 0, left, same)
    last = jnp.where(chan == devices - 1, right, same)
    pos = jnp.concatenate([first, same, last], axis=0)
    hot = (pos[:, :, None] == jnp.arange(slots + REACH, dtype=jnp.int32)).astype(BF16)
    return jnp.stack(send_pos), hot


def send_faces(faces, chan, regions, devices):
    got = []
    for source in range(devices):
        other = (source + devices // 2) % devices
        pairs = [(r * devices + source, (r + 1) * devices) for r in range(regions - 1)]
        pairs += [(r * devices + other, r * devices - 1) for r in range(1, regions)]
        got.append(lax.ppermute(jnp.where(chan == source, faces[0], faces[1]), ("region", "chan"), pairs))
    swapped = got[devices // 2 :] + got[: devices // 2]
    return jnp.where(chan == devices - 1, jnp.stack(swapped), jnp.stack(got))


def body(point_feats, destination, voxel_slot, adjacency, active_count, conv_weight, down_weight):
    regions = lax.axis_size("region")
    region = lax.axis_index("region")
    devices = lax.axis_size("chan")
    chan = lax.axis_index("chan")
    slots = adjacency.shape[0]
    points = point_feats.shape[1]
    cells = slots * 512
    per = points // regions

    slot = voxel_slot // 512
    inside = voxel_slot % 512
    code = ((inside // 8) * slots + slot) * 8 + inside % 8
    key, order = lax.sort(
        (destination * cells + code, jnp.arange(points, dtype=jnp.int32)), num_keys=1, is_stable=False
    )
    ids = lax.all_to_all((key % cells).reshape(regions, per // LANES, LANES), "region", 0, 0, tiled=True)
    moved = permute(point_feats, order.reshape(points // LANES, LANES), regions)
    moved = lax.all_to_all(moved, "region", 0, 0, tiled=True)

    taps = conv_weight.transpose(2, 3, 4, 0, 1).reshape(9, 3, conv_weight.shape[0], -1)
    taps = lax.all_gather(taps, "chan", axis=2, tiled=True)
    weights = banded(taps.transpose(0, 2, 1, 3).reshape(9, taps.shape[2], -1))
    down = lax.all_gather(down_weight, "chan", axis=1, tiled=True)
    down = down.transpose(0, 2, 3, 4, 1).reshape(down.shape[0], -1)

    send_pos, hot = links(adjacency, region, regions, chan, devices)
    planes, faces = voxels(moved, ids, send_pos, slots, devices)
    remote = send_faces(faces, chan, regions, devices)
    grid = lax.all_to_all(planes, "chan", 0, 0, tiled=True)
    coarse = convolve(active_count, grid, remote, hot, weights, down)
    coarse = lax.all_to_all(coarse, "chan", 0, 0, tiled=True)
    return finish(coarse, slots)


def solution(mesh):
    return jax.shard_map(
        body,
        mesh=mesh,
        in_specs=(
            P("chan", "region"),
            P("region"),
            P("region"),
            P("region", None),
            P("region"),
            P("chan", None, None, None, None),
            P(None, "chan", None, None, None),
        ),
        out_specs=P("region", "chan"),
        check_vma=False,
    )
```

time: 966 us -> 132 us (0.14); the launches traced: 952 us -> 131 us
  local copies, waits for them, and re-layouts: 539 us -> 7.14 us
  other arithmetic: 245 us -> 14.2 us
  waiting for transfers between devices: 87.2 us -> 3.88 us
  Pallas kernels: 0 us -> 47.3 us
  matrix products: 46.8 us -> 0 us
  blocking collectives: 0 us -> 33.1 us
  between operations: 15.1 us -> 0.94 us
    scatter x26 -> x0, local copies, waits for them, and re-layouts: 245 us -> none  [body(): padded = padded.at[(slice(None), slice(None)) + target].set(slab)]
    scatter-add x2 -> x0, other arithmetic: 180 us -> none  [the longest x1 94.4 us: splat(): totals = jnp.zeros((channels, slot_count * 512), jnp.float32).at[:, voxel...]
    gather x29 -> x0, local copies, waits for them, and re-layouts: 174 us -> none  [the longest x1 90.5 us: body(): jnp.take(voxel_slot, sorted_order)[None, :]]
    pallas_call x0 -> x5, Pallas kernels: none -> 47.3 us  [the longest x1 20.2 us: permute(): pl.pallas_call(functools.partial(permute_kernel, depth), out_shape=jax.Sh...]
    conv_general_dilated x2 -> x0, matrix products: 46.8 us -> none  [the longest x1 44.1 us: body(): lax.conv_general_dilated(padded, conv_weight, (1, 1, 1), 'VALID', dimensi...]
    reduce_scatter x1 -> x0, waiting for transfers between devices: 45.8 us -> none  [body(): lax.psum_scatter(partial_sums, 'chan', scatter_dimension=1, tiled=True)]
    select_n x26 -> x0, local copies, waits for them, and re-layouts: 42.6 us -> none  [body(): slab = jnp.take(slab_tables[number], picked, axis=0)]
    all_gather x1 -> x0, waiting for transfers between devices: 41.4 us -> none  [body(): full_grid = lax.all_gather(shard_grid, 'chan', axis=1, tiled=True)]
  transfers between devices with their start and end apart: 6 -> 7, of which waited for: 2 -> 1; matrix products, arithmetic and copies ran while one was open for 24% -> 5% of each run, Pallas kernels for 0% -> 17%
where the time goes in v1:
time: 132 us; the launch traced here: 131 us
  Pallas kernels  47.3 us (36%)
  blocking collectives  33.1 us (25%)
  starting transfers between devices  24.2 us (18%)
  other arithmetic  14.2 us (11%)
  local copies, waits for them, and re-layouts  7.14 us (5%)
  waiting for transfers between devices  3.88 us (3%)
    pallas_call x1, Pallas kernels, permute(): pl.pallas_call(functools.partial(permute_kernel, depth), out_shape=jax.Sh...  20.2 us
    all_gather x1, blocking collectives, body(): down = lax.all_gather(down_weight, 'chan', axis=1, tiled=True)  18 us
    pallas_call x1, Pallas kernels, voxels(): pl.pallas_call(functools.partial(voxel_kernel, slots), out_shape=(jax.Sha...  15.8 us
    all_to_all x1, blocking collectives, body(): coarse = lax.all_to_all(coarse, 'chan', 0, 0, tiled=True)  8.42 us
    pallas_call x1, Pallas kernels, convolve(): pl.pallas_call(functools.partial(conv_kernel, slots), out_shape=jax.Shape...  7.57 us
    ppermute x4, starting transfers between devices, send_faces(): lax.ppermute(jnp.where(chan == source, faces[0], faces[1]), ('region', 'c...  7.37 us
    all_to_all x1, starting transfers between devices, body(): lax.all_to_all((key % cells).reshape(regions, per // LANES, LANES), 'regi...  7.25 us
    all_gather x1, blocking collectives, body(): taps = lax.all_gather(taps, 'chan', axis=2, tiled=True)  6.75 us
  transfers between devices with their start and end apart: 7, of which 1 were waited for; matrix products, arithmetic and copies ran while one was open for 5% of the time, Pallas kernels for 17%

profile of v1, /device:TPU:0, one launch (start us, length us, event | category | flops | bytes accessed | tf_op | source)
XLA Modules:
  0.0 130.8 jit_solution(7568116251531192770)
XLA Ops:
  0.0 0.0 copy-start.6
  0.0 1.0 fusion.11
  1.1 6.4 %sort.15 = (s32[16384]{0:T(1024)S(1)}, s32[16384]{0:T(1024)S(1)}) sort(s32[16384]{0:T(1024)S(1)} %fusion.11, s32[16384]{0:T(1024)S(1)} %iota.26), dimensions={0}, to_apply=%region_0.1 | sort | flops 229376 | bytes 262144 | tf_op jit(solution)/shard_map/sort | solution.py:379
  7.5 0.7 add_select_fusion
  8.2 7.3 %all-to-all-start.1 = ((s32[8,16,128]{2,1,0:T(8,128)}), s32[8,16,128]{2,1,0:T(8,128)S(1)}, u32[]{:S(2)}, u32[]{:S(2)}) async-start(s32[8,16,128]{2,1,0:T(8,128)} %bitcast.1), calls=%async_computation.1 | async-start | bytes 131072 | tf_op jit(solution)/shard_map/all_to_all | solution.py:382
  15.4 0.7 compare_select_fusion
  16.2 0.0 copy-start.4
  16.2 1.0 copy-done.4
  17.2 20.2 %permute.1 = bf16[8,16,16,128]{3,2,1,0:T(8,128)(2,1)} custom-call(bf16[16,16384]{1,0:T(8,128)(2,1)S(1)} %copy-done.4, s32[128,128]{1,0:T(8,128)S(1)} %bitcast.60), custom_call_target="tpu_custom_call" | custom-call | tf_op jit(solution)/shard_map/permute/pallas_call | solution.py:65
  37.5 0.0 copy-start.7
  37.5 0.1 convert_reduce_fusion.3
  37.6 0.0 all-to-all-done.1.ids
  37.6 6.0 %all-to-all-start = ((bf16[8,16,16,128]{3,2,1,0:T(8,128)(2,1)}), bf16[8,16,16,128]{3,2,1,0:T(8,128)(2,1)S(1)}, u32[]{:S(2)}, u32[]{:S(2)}) async-start(bf16[8,16,16,128]{3,2,1,0:T(8,128)(2,1)} %permute.1), calls=%async_computation | async-start | bytes 1048576 | tf_op jit(solution)/shard_map/all_to_all | solution.py:384
  43.6 0.0 copy-done.6
  43.6 6.8 %all_gather.6 = bf16[9,3,64,64]{3,2,1,0:T(8,128)(2,1)S(1)} all-gather(bf16[9,3,16,64]{3,2,1,0:T(8,128)(2,1)S(1)} %bitcast.64), channel_id=1, replica_groups=mesh['region'=8,'chan'=4] {'chan'}, dimensions={2}, use_global_device_ids=true | all-gather | bytes 276480 | tf_op jit(solution)/shard_map/all_gather | solution.py:387
  50.4 0.2 copy.24
  50.6 0.2 copy.25.weights
  50.9 0.0 copy-done.7
  50.9 2.6 %convert_reduce_fusion = s32[17,8]{1,0:T(8,128)S(1)} fusion(s32[8,16,128]{2,1,0:T(8,128)S(1)} %all-to-all-done.1.ids, s32[17]{0:T(128)S(1)} %iota_multiply_fusion), kind=kLoop, calls=%fused_computation | loop fusion | flops 835448 | bytes 66148 | tf_op jit(solution)/shard_map/reduce_sum | solution.py:147
  53.5 0.1 subtract_reduce_fusion
  53.6 0.1 copy.23.hops
  53.7 3.9 %all-to-all-done.feats = bf16[8,16,16,128]{3,2,1,0:T(8,128)(2,1)S(1)} async-done(((bf16[8,16,16,128]{3,2,1,0:T(8,128)(2,1)}), bf16[8,16,16,128]{3,2,1,0:T(8,128)(2,1)S(1)}, u32[]{:S(2)}, u32[]{:S(2)}) %all-to-all-start) | async-done | bytes 524320 | tf_op jit(solution)/shard_map/all_to_all | solution.py:384
  57.6 15.8 %voxels.1 = (bf16[4,4,512,128]{3,2,1,0:T(8,128)(2,1)S(1)}, bf16[2,8,16,128]{3,2,1,0:T(8,128)(2,1)S(1)}) custom-call(bf16[8,16,16,128]{3,2,1,0:T(8,128)(2,1)S(1)} %all-to-all-done.feats, s32[8,16,128]{2,1,0:T(8,128)S(1)} %all-to-all-done.1.ids, s32[16,8]{1,0:T(8,128)S(1)} %get-tuple-element.34.first, s32[16,8]{1,0:T(8,128)S(1)} %get-tuple-element.18.last, ...), custom_call_target="tpu_custom_call" | custom-call | tf_op jit(solution)/shard_map/voxels/pallas_call | solution.py:151
  73.4 0.0 copy-start.2
  73.4 1.3 %copy-done.2 = bf16[4,4,512,128]{3,2,1,0:T(8,128)(2,1)} copy-done((bf16[4,4,512,128]{3,2,1,0:T(8,128)(2,1)}, bf16[4,4,512,128]{3,2,1,0:T(8,128)(2,1)S(1)}, u32[]{:S(2)}) %copy-start.2) | copy-done | bytes 2097176
  74.8 3.6 %all-to-all-start.2 = ((bf16[4,4,512,128]{3,2,1,0:T(8,128)(2,1)}), bf16[4,4,512,128]{3,2,1,0:T(8,128)(2,1)S(1)}, u32[]{:S(2)}, u32[]{:S(2)}) async-start(bf16[4,4,512,128]{3,2,1,0:T(8,128)(2,1)} %copy-done.2), calls=%async_computation.2 | async-start | bytes 4194304 | tf_op jit(solution)/shard_map/all_to_all | solution.py:395
  78.4 0.5 fusion.2
  78.9 0.4 convert_reduce_fusion.1
  79.3 0.4 convert_reduce_fusion.2
  79.7 0.2 concatenate.8
  79.9 0.3 fusion.hot
  80.3 4.1 %collective-permute-start.2 = (bf16[8,16,128]{2,1,0:T(8,128)(2,1)S(1)}, bf16[8,16,128]{2,1,0:T(8,128)(2,1)S(1)}, u32[]{:S(2)}, u32[]{:S(2)}) collective-permute-start(bf16[8,16,128]{2,1,0:T(8,128)(2,1)S(1)} %get-tuple-element.20), channel_id=1, source_target_pairs={{0,4},{4,8},{8,12},{12,16},{16,20},{20,24},{24,28},{6,3},{10,7},{1... | collective-permute-start | bytes 98312 | tf_op jit(solution)/shard_map/ppermute | solution.py:361
  84.3 0.7 collective-permute-start.3
  85.0 1.3 collective-permute-start
  86.3 0.0 copy-start.5
  86.3 1.4 %collective-permute-start.1 = (bf16[8,16,128]{2,1,0:T(8,128)(2,1)S(1)}, bf16[8,16,128]{2,1,0:T(8,128)(2,1)}, u32[]{:S(2)}, u32[]{:S(2)}) collective-permute-start(bf16[8,16,128]{2,1,0:T(8,128)(2,1)S(1)} %get-tuple-element.22), channel_id=1, source_target_pairs={{3,4},{7,8},{11,12},{15,16},{19,20},{23,24},{27,28},{5,3},{9,7},{1... | collective-permute-start | bytes 98312 | tf_op jit(solution)/shard_map/ppermute | solution.py:361
  87.6 18.0 %all_gather.7 = bf16[128,64,2,2,2]{0,1,4,3,2:T(8,128)(2,1)S(1)} all-gather(bf16[128,16,2,2,2]{0,1,4,3,2:T(8,128)(2,1)S(1)} %copy.26), channel_id=1, replica_groups=mesh['region'=8,'chan'=4] {'chan'}, dimensions={1}, use_global_device_ids=true | all-gather | bytes 163840 | tf_op jit(solution)/shard_map/all_gather | solution.py:389
  105.6 0.1 copy.27.down
  106.4 0.0 copy-start.3
  106.4 1.1 copy-done.3
  107.5 2.1 %banded.1.weights = bf16[9,384,256]{2,1,0:T(8,128)(2,1)S(1)} custom-call(bf16[4,384,192]{2,1,0:T(8,128)(2,1)S(1)} %copy-done.3, bf16[9,64,192]{2,1,0:T(8,128)(2,1)S(1)} %copy.25.weights), custom_call_target="tpu_custom_call" | custom-call | tf_op jit(solution)/shard_map/banded/pallas_call | solution.py:189
  109.5 0.0 copy-start
  109.6 1.2 copy-done
  110.8 0.0 collective-permute-done.2
  110.8 0.0 collective-permute-done.3
  110.8 0.0 collective-permute-done
  110.8 0.0 collective-permute-done.1
  110.8 0.9 maximum_select_fusion.remote
  111.7 0.0 all-to-all-done.2.grid
  111.7 0.0 copy-done.5
  111.7 0.0 copy-start.1
  111.7 1.5 %copy-done.1 = bf16[9,384,256]{2,1,0:T(8,128)(2,1)S(1)} copy-done((bf16[9,384,256]{2,1,0:T(8,128)(2,1)S(1)}, bf16[9,384,256]{2,1,0:T(8,128)(2,1)}, u32[]{:S(2)}) %copy-start.1) | copy-done | bytes 1769496
  113.2 7.6 %convolve.1 = bf16[4,32,1024]{2,1,0:T(8,128)(2,1)S(1)} custom-call(s32[1]{0:T(128)S(6)} %copy.28.active, bf16[4,4,512,128]{3,2,1,0:T(8,128)(2,1)S(1)} %all-to-all-done.2.grid, bf16[4,8,16,128]{3,2,1,0:T(8,128)(2,1)S(1)} %maximum_select_fusion.remote, bf16[27,64,80]{2,1,0:T(8,128)(2,1)S(1)} %fusion.hot, bf16[512,256]{1,0:T(8,128)(2,1)S(1)} %copy-done.5, ...), custom_call_target="tpu_custom_call" | custom-call | tf_op jit(solution)/shard_map/convolve/pallas_call | solution.py:283
  120.7 8.4 %all_to_all.20.data = bf16[4,32,1024]{2,1,0:T(8,128)(2,1)S(1)} all-to-all(bf16[4,32,1024]{2,1,0:T(8,128)(2,1)S(1)} %convolve.1), channel_id=1, replica_groups=mesh['region'=8,'chan'=4] {'chan'}, dimensions={0} | all-to-all | bytes 524288 | tf_op jit(solution)/shard_map/all_to_all | solution.py:397
  129.2 1.7 %finish.1 = bf16[64,2048]{1,0:T(8,128)(2,1)} custom-call(bf16[4,32,1024]{2,1,0:T(8,128)(2,1)S(1)} %all_to_all.20.data), custom_call_target="tpu_custom_call" | custom-call | tf_op jit(solution)/shard_map/finish/pallas_call | solution.py:311
  (13 shorter events, 0.1 us)
Async XLA Ops:
  0.0 43.6 %copy-start.6 = (bf16[16,64,3,3,3]{1,0,4,3,2:T(8,128)(2,1)S(1)}, bf16[16,64,3,3,3]{1,0,4,3,2:T(8,128)(2,1)}, u32[]{:S(2)}) copy-start(bf16[16,64,3,3,3]{1,0,4,3,2:T(8,128)(2,1)} %param.14) | copy-start | bytes 165892
  8.2 29.4 %all-to-all-start.1 = ((s32[8,16,128]{2,1,0:T(8,128)}), s32[8,16,128]{2,1,0:T(8,128)S(1)}, u32[]{:S(2)}, u32[]{:S(2)}) async-start(s32[8,16,128]{2,1,0:T(8,128)} %bitcast.1), calls=%async_computation.1 | async-start | bytes 131072 | tf_op jit(solution)/shard_map/all_to_all | solution.py:382
  16.2 1.0 copy-start.4
  37.5 13.4 %copy-start.7 = (bf16[128,16,2,2,2]{0,4,3,2,1:T(2,128)(2,1)S(1)}, bf16[128,16,2,2,2]{0,4,3,2,1:T(2,128)(2,1)}, u32[]{:S(2)}) copy-start(bf16[128,16,2,2,2]{0,4,3,2,1:T(2,128)(2,1)} %param.15) | copy-start | bytes 98308
  37.6 20.0 %all-to-all-start = ((bf16[8,16,16,128]{3,2,1,0:T(8,128)(2,1)}), bf16[8,16,16,128]{3,2,1,0:T(8,128)(2,1)S(1)}, u32[]{:S(2)}, u32[]{:S(2)}) async-start(bf16[8,16,16,128]{3,2,1,0:T(8,128)(2,1)} %permute.1), calls=%async_computation | async-start | bytes 1048576 | tf_op jit(solution)/shard_map/all_to_all | solution.py:384
  73.4 1.4 %copy-start.2 = (bf16[4,4,512,128]{3,2,1,0:T(8,128)(2,1)}, bf16[4,4,512,128]{3,2,1,0:T(8,128)(2,1)S(1)}, u32[]{:S(2)}) copy-start(bf16[4,4,512,128]{3,2,1,0:T(8,128)(2,1)S(1)} %get-tuple-element.11) | copy-start | bytes 6291460
  74.8 36.9 %all-to-all-start.2 = ((bf16[4,4,512,128]{3,2,1,0:T(8,128)(2,1)}), bf16[4,4,512,128]{3,2,1,0:T(8,128)(2,1)S(1)}, u32[]{:S(2)}, u32[]{:S(2)}) async-start(bf16[4,4,512,128]{3,2,1,0:T(8,128)(2,1)} %copy-done.2), calls=%async_computation.2 | async-start | bytes 4194304 | tf_op jit(solution)/shard_map/all_to_all | solution.py:395
  80.3 30.5 %collective-permute-start.2 = (bf16[8,16,128]{2,1,0:T(8,128)(2,1)S(1)}, bf16[8,16,128]{2,1,0:T(8,128)(2,1)S(1)}, u32[]{:S(2)}, u32[]{:S(2)}) collective-permute-start(bf16[8,16,128]{2,1,0:T(8,128)(2,1)S(1)} %get-tuple-element.20), channel_id=1, source_target_pairs={{0,4},{4,8},{8,12},{12,16},{16,20},{20,24},{24,28},{6,3},{10,7},{1... | collective-permute-start | bytes 98312 | tf_op jit(solution)/shard_map/ppermute | solution.py:361
  84.3 26.5 %collective-permute-start.3 = (bf16[8,16,128]{2,1,0:T(8,128)(2,1)S(1)}, bf16[8,16,128]{2,1,0:T(8,128)(2,1)S(1)}, u32[]{:S(2)}, u32[]{:S(2)}) collective-permute-start(bf16[8,16,128]{2,1,0:T(8,128)(2,1)S(1)} %get-tuple-element.21), channel_id=1, source_target_pairs={{1,4},{5,8},{9,12},{13,16},{17,20},{21,24},{25,28},{7,3},{11,7},{1... | collective-permute-start | bytes 98312 | tf_op jit(solution)/shard_map/ppermute | solution.py:361
  85.0 25.8 %collective-permute-start = (bf16[8,16,128]{2,1,0:T(8,128)(2,1)S(1)}, bf16[8,16,128]{2,1,0:T(8,128)(2,1)}, u32[]{:S(2)}, u32[]{:S(2)}) collective-permute-start(bf16[8,16,128]{2,1,0:T(8,128)(2,1)S(1)} %get-tuple-element.19), channel_id=1, source_target_pairs={{2,4},{6,8},{10,12},{14,16},{18,20},{22,24},{26,28},{4,3},{8,7},{1... | collective-permute-start | bytes 98312 | tf_op jit(solution)/shard_map/ppermute | solution.py:361
  86.3 25.4 %copy-start.5 = (bf16[512,256]{1,0:T(8,128)(2,1)S(1)}, bf16[512,256]{1,0:T(8,128)(2,1)}, u32[]{:S(2)}) copy-start(bf16[512,256]{1,0:T(8,128)(2,1)} %constant.140.clone.pick) | copy-start | bytes 786436
  86.3 24.5 %collective-permute-start.1 = (bf16[8,16,128]{2,1,0:T(8,128)(2,1)S(1)}, bf16[8,16,128]{2,1,0:T(8,128)(2,1)}, u32[]{:S(2)}, u32[]{:S(2)}) collective-permute-start(bf16[8,16,128]{2,1,0:T(8,128)(2,1)S(1)} %get-tuple-element.22), channel_id=1, source_target_pairs={{3,4},{7,8},{11,12},{15,16},{19,20},{23,24},{27,28},{5,3},{9,7},{1... | collective-permute-start | bytes 98312 | tf_op jit(solution)/shard_map/ppermute | solution.py:361
  106.4 1.1 copy-start.3
  109.5 1.2 copy-start
  111.7 1.5 %copy-start.1 = (bf16[9,384,256]{2,1,0:T(8,128)(2,1)S(1)}, bf16[9,384,256]{2,1,0:T(8,128)(2,1)}, u32[]{:S(2)}) copy-start(bf16[9,384,256]{2,1,0:T(8,128)(2,1)} %copy-done) | copy-start | bytes 5308420

commit v2 on v1

v2 whole, which is shorter than its diff:
```python
import functools

import jax
import jax.numpy as jnp
import numpy as np
from jax import lax
from jax.experimental import pallas as pl
from jax.experimental.pallas import tpu as pltpu
from jax.sharding import PartitionSpec as P

OFFSETS = [
    (first, second, third)
    for first in (-1, 0, 1)
    for second in (-1, 0, 1)
    for third in (-1, 0, 1)
    if (first, second, third) != (0, 0, 0)
]
LANES = 128
REACH = 16
F32 = jnp.float32
BF16 = jnp.bfloat16
NT = (((1,), (1,)), ((), ()))
VMEM = pl.BlockSpec(memory_space=pltpu.VMEM)
SMEM = pl.BlockSpec(memory_space=pltpu.SMEM)


def mm(a, b):
    return jnp.dot(a, b, preferred_element_type=F32)


def params():
    return pltpu.CompilerParams(vmem_limit_bytes=48 * 1024 * 1024)


ID_ROWS = 16


def permute_kernel(depth, width, cells, feats, order, keys, ready, out, stack):
    channels, points = feats.shape
    high = points // depth
    for part in range(high):
        stack[part * channels : (part + 1) * channels, :] = feats[:, part * depth : (part + 1) * depth]
    regions = out.shape[0]
    blocks = points // regions // LANES
    tiles = (out.shape[1] - blocks) // 2
    count = width // LANES

    def step(at, _):
        wanted = order[pl.ds(at * count, count), :]
        wanted = jnp.concatenate([wanted[i : i + 1] for i in range(count)], axis=1)
        low = (wanted & (depth - 1)).astype(jnp.int16)
        top = wanted // depth
        hot = lax.broadcasted_iota(jnp.int16, (depth, width), 0) == low
        hot = jnp.where(hot, jnp.ones((), BF16), jnp.zeros((), BF16))
        found = mm(stack[...], hot)
        picked = jnp.zeros((channels, width), F32)
        for part in range(high):
            picked = jnp.where(top == part, found[part * channels : (part + 1) * channels], picked)
        picked = picked.astype(BF16)
        for part in range(count):
            tile = at * count + part
            out[tile // blocks, tile % blocks] = picked[:, part * LANES : (part + 1) * LANES]
        return 0

    lax.fori_loop(0, points // width, step, 0)
    for target in range(regions):
        for tile in range(tiles):
            begin = target * blocks + tile * ID_ROWS
            rows = min(ID_ROWS, blocks - tile * ID_ROWS)
            code = lax.rem(keys[begin : begin + rows, :], cells)
            if rows < ID_ROWS:
                code = jnp.concatenate([code, jnp.zeros((ID_ROWS - rows, LANES), jnp.int32)], axis=0)
            out[target, blocks + tile] = (code >> 8).astype(F32).astype(BF16)
            out[target, blocks + tiles + tile] = (code & 255).astype(F32).astype(BF16)


def permute(feats, order, keys, ready, regions, cells):
    channels, points = feats.shape
    depth, width = 512, 1024
    blocks = points // regions // LANES
    tiles = -(-blocks // ID_ROWS)
    return pl.pallas_call(
        functools.partial(permute_kernel, depth, width, cells),
        out_shape=jax.ShapeDtypeStruct((regions, blocks + 2 * tiles, channels, LANES), BF16),
        in_specs=[VMEM, VMEM, VMEM, pl.BlockSpec(memory_space=pl.ANY)],
        out_specs=VMEM,
        scratch_shapes=[pltpu.VMEM((points // depth * channels, depth), BF16)],
        compiler_params=params(),
        name="permute",
    )(feats, order, keys, ready)


WINDOW = 256
GROUP = 8
STATIC = 2


def decode(feats, ids):
    chunks, total, _, _ = feats.shape
    tiles = ids.shape[1] // ID_ROWS
    blocks = total - 2 * tiles
    for chunk in range(chunks):
        for tile in range(tiles):
            upper = feats[chunk, blocks + tile].astype(F32)
            lower = feats[chunk, blocks + tiles + tile].astype(F32)
            ids[chunk, tile * ID_ROWS : (tile + 1) * ID_ROWS, :] = (upper * 256.0 + lower).astype(jnp.int32)


def window_mean(number, feats, ids, first, last, hops, acc):
    chunks, total, channels, _ = feats.shape
    groups = chunks // GROUP
    blocks = total - 2 * (ids.shape[1] // ID_ROWS)

    def product(group, steps):
        sides = []
        rows = []
        for at in steps:
            for member in range(GROUP):
                chunk = group * GROUP + member
                block = first[number, chunk] + at
                valid = block < last[number, chunk]
                block = jnp.minimum(block, blocks - 1)
                code = ids[chunk, pl.ds(block, 1), :]
                cell = code & 7
                rows.append(jnp.where(valid, (code >> 3) - number * WINDOW, -1))
                values = feats[chunk, block].astype(F32)
                mask = [cell == k for k in range(8)]
                side = [jnp.where(m, values, 0.0).astype(BF16) for m in mask]
                side += [jnp.broadcast_to(jnp.where(m, 1.0, 0.0), (channels, LANES)).astype(BF16) for m in mask]
                sides.append(jnp.concatenate(side, axis=0))
        side = jnp.concatenate(sides, axis=1)
        row = jnp.concatenate(rows, axis=1).astype(jnp.int16)
        hot = lax.broadcasted_iota(jnp.int16, (WINDOW, len(steps) * GROUP * LANES), 0) == row
        hot = jnp.where(hot, jnp.ones((), BF16), jnp.zeros((), BF16))
        return lax.dot_general(hot, side, NT, preferred_element_type=F32)

    def one_group(group, start):
        def step(at, _):
            acc[...] += product(group, [at])
            return 0

        lax.fori_loop(start, hops[number, group], step, 0)

    if groups == 1:
        acc[...] = product(0, list(range(STATIC)))
        one_group(0, STATIC)
    else:
        acc[...] = jnp.zeros_like(acc)

        def each(group, _):
            one_group(group, 0)
            return 0

        lax.fori_loop(0, groups, each, 0)
    return (acc[:, :LANES] / jnp.maximum(acc[:, LANES:], 1.0)).astype(BF16)


def far_kernel(chan, feats, first, last, hops, out, ids, acc):
    decode(feats, ids)
    begin = 2 * (chan[0] ^ 2) + 7
    parts = out.shape[1] // WINDOW
    for plane in range(4):
        for part in range(parts):
            number = lax.rem(begin + plane, 8) * parts + part
            out[plane, part * WINDOW : (part + 1) * WINDOW, :] = window_mean(number, feats, ids, first, last, hops, acc)


def near_kernel(slots, chan, feats, first, last, hops, far, send_pos, out, faces, ids, acc, planes):
    decode(feats, ids)
    partner = chan[0] ^ 2
    begin = 2 * partner + 7
    parts = far.shape[1] // WINDOW
    planes[0:4] = far[...]
    for plane in range(4, 8):
        for part in range(parts):
            number = lax.rem(begin + plane, 8) * parts + part
            planes[plane, part * WINDOW : (part + 1) * WINDOW, :] = window_mean(
                number, feats, ids, first, last, hops, acc
            )
    for place, flip in enumerate((3, 1, 0)):
        shift = 2 * ((chan[0] ^ flip) - partner) + 8
        for plane in range(4):
            out[place, plane] = planes[lax.rem(shift + plane, 8)]
    for side in range(2):
        hot = lax.broadcasted_iota(jnp.int32, (REACH, slots), 0) == send_pos[side : side + 1, :]
        hot = jnp.where(hot, 1.0, 0.0).astype(BF16)
        face = planes.at[lax.rem((7, 8)[side] - begin + 16, 8)]
        for j in range(8):
            faces[side, j] = mm(hot, face[j * slots : (j + 1) * slots, :]).astype(BF16)


def ranges(moved, tiles, slots):
    chunks, total, _, _ = moved.shape
    blocks = total - 2 * tiles
    ends = moved[:, blocks:, :, :: LANES - 1].astype(F32)
    ends = ends[:, :tiles] * 256.0 + ends[:, tiles:]
    ends = ends.reshape(chunks, tiles * ID_ROWS, 2)[:, :blocks].astype(jnp.int32)
    windows = slots * 64 // WINDOW
    bounds = (jnp.arange(windows, dtype=jnp.int32) * (WINDOW * 8))[:, None, None]
    first = jnp.sum((ends[None, :, :, 1] < bounds).astype(jnp.int32), axis=2)
    last = jnp.sum((ends[None, :, :, 0] < bounds + WINDOW * 8).astype(jnp.int32), axis=2)
    hops = jnp.max((last - first).reshape(windows, chunks // GROUP, GROUP), axis=2)
    return first, last, hops


def far_voxels(chan, moved, bounds, slots, tiles):
    return pl.pallas_call(
        far_kernel,
        out_shape=jax.ShapeDtypeStruct((4, 8 * slots, LANES), BF16),
        in_specs=[SMEM, VMEM, SMEM, SMEM, SMEM],
        out_specs=VMEM,
        scratch_shapes=[
            pltpu.VMEM((moved.shape[0], tiles * ID_ROWS, LANES), jnp.int32),
            pltpu.VMEM((WINDOW, 2 * LANES), F32),
        ],
        compiler_params=params(),
        cost_estimate=pl.CostEstimate(flops=4_000_000_000, bytes_accessed=1_200_000, transcendentals=0),
        name="far_voxels",
    )(chan, moved, *bounds)


def near_voxels(chan, moved, bounds, far, send_pos, slots, tiles):
    return pl.pallas_call(
        functools.partial(near_kernel, slots),
        out_shape=(
            jax.ShapeDtypeStruct((3, 4, 8 * slots, LANES), BF16),
            jax.ShapeDtypeStruct((2, 8, REACH, LANES), BF16),
        ),
        in_specs=[SMEM, VMEM, SMEM, SMEM, SMEM, VMEM, VMEM],
        out_specs=(VMEM, VMEM),
        scratch_shapes=[
            pltpu.VMEM((moved.shape[0], tiles * ID_ROWS, LANES), jnp.int32),
            pltpu.VMEM((WINDOW, 2 * LANES), F32),
            pltpu.VMEM((8, 8 * slots, LANES), BF16),
        ],
        compiler_params=params(),
        cost_estimate=pl.CostEstimate(flops=4_000_000_000, bytes_accessed=3_000_000, transcendentals=0),
        name="near_voxels",
    )(chan, moved, *bounds, far, send_pos)


def spread_matrix():
    spread = np.zeros((4, 384, 192), np.float32)
    for k in range(4):
        for e in range(3):
            cell = k + e
            for channel in range(64):
                source, inner = divmod(channel, 16)
                if 1 <= cell <= 4:
                    row = source * 64 + (cell - 1) * 16 + inner
                else:
                    row = 256 + (cell // 5) * 64 + source * 16 + inner
                spread[k, row, e * 64 + channel] = 1
    return spread


def weight_kernel(chan, spread, own, one, two, three, out, down):
    every = (own, one, two, three)
    columns = lax.broadcasted_iota(jnp.int32, (192, 192), 1) ^ (chan[0] * 16)
    turn = jnp.where(lax.broadcasted_iota(jnp.int32, (192, 192), 0) == columns, 1.0, 0.0).astype(BF16)
    for ab in range(9):
        taps = jnp.concatenate([ref[ab] for ref in every], axis=0)
        taps = mm(taps, turn).astype(BF16)
        for k in range(4):
            out[ab, :, k * 64 : (k + 1) * 64] = lax.dot_general(
                spread[k], taps, NT, preferred_element_type=F32
            ).astype(BF16)
    outputs = down.shape[0]
    total = jnp.zeros((outputs, 512), F32)
    rows = lax.broadcasted_iota(jnp.int32, (128, 512), 0)
    place = (rows >> 4) * 64 + (rows & 15)
    for source, ref in enumerate(every):
        part = ref[9:, :, 0:128].reshape(outputs, 128)
        move = lax.broadcasted_iota(jnp.int32, (128, 512), 1) == place + source * 16
        total += mm(part, jnp.where(move, 1.0, 0.0).astype(BF16))
    down[...] = total.astype(BF16)


def prepare(chan, own, others, outputs):
    return pl.pallas_call(
        weight_kernel,
        out_shape=(
            jax.ShapeDtypeStruct((9, 384, 256), BF16),
            jax.ShapeDtypeStruct((outputs, 512), BF16),
        ),
        in_specs=[SMEM] + [VMEM] * 5,
        out_specs=(VMEM, VMEM),
        compiler_params=params(),
        cost_estimate=pl.CostEstimate(flops=2_000_000_000, bytes_accessed=3_000_000, transcendentals=0),
        name="prepare",
    )(chan, jnp.asarray(spread_matrix(), BF16), own, *others)


def halo_matrix():
    pick = np.zeros((512, 256), np.float32)
    for group, cell in enumerate((7, 0, 3, 4)):
        for source in range(4):
            for inner in range(16):
                pick[source * 128 + cell * 16 + inner, group * 64 + source * 16 + inner] = 1
    return pick


def conv_kernel(slots, chan, active, near, one, two, three, r0, r1, r2, r3, hot, pick, weights, down, *rest):
    grid = (near.at[2], one, two, three)
    remote = (r0, r1, r2, r3)
    out, table, padded, stacked, answer = rest
    rows = slots * 8
    extra = REACH
    total = slots + extra
    low = lax.broadcasted_iota(jnp.int32, (slots, LANES), 1) < 64

    def arrange(parts, plane, j, at, count):
        for half in range(2):
            cut = slice(half * 64, half * 64 + 64)
            for pair in range(2):
                both = jnp.concatenate([parts[2 * pair][:, cut], parts[2 * pair + 1][:, cut]], axis=1)
                table[plane, j, at : at + count, half * 384 + pair * 128 : half * 384 + pair * 128 + 128] = both

    for plane in range(4):
        whole = jnp.concatenate([grid[source][plane] for source in range(4)], axis=1)
        edge = mm(whole, pick[...]).astype(BF16)
        for j in range(8):
            arrange([grid[s][plane, j * slots : (j + 1) * slots, :] for s in range(4)], plane, j, 0, slots)
            table[plane, j, 0:slots, 256:384] = edge[j * slots : (j + 1) * slots, :128]
            table[plane, j, 0:slots, 640:768] = edge[j * slots : (j + 1) * slots, 128:]
    for plane in (0, 3):
        for j in range(8):
            parts = [remote[s][j] for s in range(4)]
            arrange(parts, plane, j, slots, extra)
            edge = mm(jnp.concatenate(parts, axis=1), pick[...]).astype(BF16)
            table[plane, j, slots:total, 256:384] = edge[:, :128]
            table[plane, j, slots:total, 640:768] = edge[:, 128:]

    for plane in range(4):
        base = (0, 9, 9, 18)[plane]
        used = total if plane in (0, 3) else slots
        for jj in range(10):
            dy, j = ((-1, 7) if jj == 0 else (1, 0) if jj == 9 else (0, jj - 1))
            at = base + (dy + 1) * 3
            source = table[plane, j, 0:used, :]
            if plane in (1, 2) and dy == 0:
                own = source
            else:
                own = mm(hot[at + 1, :, 0:used], source).astype(BF16)
            near = source[:, 256:384]
            down_edge = mm(hot[at, :, 0:used], near).astype(BF16)
            up_edge = mm(hot[at + 2, :, 0:used], near).astype(BF16)
            kept = own[:, 640:768]
            padded[plane, jj, :, 0:256] = own[:, 0:256]
            padded[plane, jj, :, 256:384] = jnp.where(low, down_edge, kept)
            padded[plane, jj, :, 384:640] = own[:, 384:640]
            padded[plane, jj, :, 640:768] = jnp.where(low, kept, up_edge)

    alive = lax.broadcasted_iota(jnp.int32, (slots, 256), 0) < active[0]
    for half in range(2):
        for a_out in range(2):
            total_sum = jnp.zeros((rows, 256), F32)
            for a in range(3):
                for b in range(3):
                    left = padded[a_out + a, b : b + 8, :, half * 384 : half * 384 + 384].reshape(rows, 384)
                    total_sum += mm(left, weights[a * 3 + b])
            for j in range(8):
                block = jnp.where(alive, jnp.maximum(total_sum[j * slots : (j + 1) * slots], 0.0), 0.0).astype(BF16)
                for kk in range(2):
                    begin = ((j // 2) * 4 + half * 2 + kk) * slots
                    place = (a_out * 2 + j % 2) * 128
                    stacked[begin : begin + slots, place : place + 128] = block[:, kk * 128 : kk * 128 + 128]

    result = lax.dot_general(down[...], stacked[...], NT, preferred_element_type=F32)
    result = jnp.maximum(result, 0.0).astype(BF16)
    devices, width, _ = out.shape
    answer[...] = result
    for flip in range(devices):
        out[flip] = answer[pl.ds(pl.multiple_of((chan[0] ^ flip) * width, width), width), :]


def convolve(chan, active, near, others, remote, hot, weights, down):
    devices = 4
    slots = near.shape[2] // 8
    outputs = down.shape[0]
    return pl.pallas_call(
        functools.partial(conv_kernel, slots),
        out_shape=jax.ShapeDtypeStruct((devices, outputs // devices, 16 * slots), BF16),
        in_specs=[SMEM] * 2 + [VMEM] * 12,
        out_specs=VMEM,
        scratch_shapes=[
            pltpu.VMEM((4, 8, slots + REACH, 768), BF16),
            pltpu.VMEM((4, 10, slots, 768), BF16),
            pltpu.VMEM((16 * slots, 512), BF16),
            pltpu.VMEM((outputs, 16 * slots), BF16),
        ],
        compiler_params=params(),
        cost_estimate=pl.CostEstimate(flops=6_000_000_000, bytes_accessed=5_000_000, transcendentals=0),
        name="convolve",
    )(chan, active, near, *others, *remote, hot, jnp.asarray(halo_matrix(), BF16), weights, down)


def final_kernel(slots, chan, own, one, two, three, out, turned):
    _, outputs, _ = own.shape
    for flip, ref in enumerate((own.at[0], one, two, three)):
        plane = chan[0] ^ flip
        for cell in range(16):
            turned[pl.ds(plane * 16 + cell, outputs, stride=64), :] = ref[
                :, cell * slots : (cell + 1) * slots
            ].astype(F32)
    for tile in range(out.shape[1] // LANES):
        out[:, tile * LANES : (tile + 1) * LANES] = turned[tile * LANES : (tile + 1) * LANES, :].T.astype(BF16)


def finish(chan, coarse, others, slots):
    outputs = coarse.shape[1]
    return pl.pallas_call(
        functools.partial(final_kernel, slots),
        out_shape=jax.ShapeDtypeStruct((slots, outputs * 64), BF16),
        in_specs=[SMEM] + [VMEM] * 4,
        out_specs=VMEM,
        scratch_shapes=[pltpu.VMEM((outputs * 64, slots), F32)],
        compiler_params=params(),
        name="finish",
    )(chan, coarse, *others)


def links(adjacency, region, regions, chan, devices):
    slots = adjacency.shape[0]
    named = adjacency.T
    linked = named < slots * regions
    owner = jnp.where(linked, named // slots, regions + 7)
    slot = named % slots
    every = jnp.arange(slots, dtype=jnp.int32)
    steps = np.array([offset[0] for offset in OFFSETS])
    send_pos = []
    place = {}
    for step in (1, -1):
        rows = np.nonzero(steps == step)[0]
        owns = owner[rows[0] : rows[-1] + 1] == region + step
        sends = jnp.any(owns, axis=0)
        rank = jnp.sum((sends[None, :] & (every[None, :] < every[:, None])).astype(jnp.int32), axis=1)
        send_pos.append(jnp.where(sends, rank, -1))
        there = slot[rows[0] : rows[-1] + 1]
        member = jnp.any(owns[:, :, None] & (there[:, :, None] == every), axis=(0, 1))
        below = jnp.sum(
            (member[None, None, :] & (every < there[:, :, None])).astype(jnp.int32), axis=2
        )
        place[step] = jnp.where(owns, slots + below, -1)
    own = jnp.where(owner == region, slot, -1)
    same = jnp.concatenate([own[9:13], every[None, :], own[13:17]], axis=0)
    left = jnp.where(owner[0:9] == region, slot[0:9], place[-1])
    right = jnp.where(owner[17:26] == region, slot[17:26], place[1])
    first = jnp.where(chan == 0, left, same)
    last = jnp.where(chan == devices - 1, right, same)
    pos = jnp.concatenate([first, same, last], axis=0)
    hot = (pos[:, :, None] == jnp.arange(slots + REACH, dtype=jnp.int32)).astype(BF16)
    return jnp.stack(send_pos), hot


def send_faces(faces, chan, regions, devices):
    got = []
    for flip in range(devices):
        other = (devices - 1) ^ flip
        pairs = [(r * devices + flip, (r + 1) * devices) for r in range(regions - 1)]
        pairs += [(r * devices + other, r * devices - 1) for r in range(1, regions)]
        got.append(lax.ppermute(jnp.where(chan == flip, faces[0], faces[1]), ("region", "chan"), pairs))
    return got


def swap(value, flip, devices):
    return lax.ppermute(value, "chan", [(source, source ^ flip) for source in range(devices)])


def body(point_feats, destination, voxel_slot, adjacency, active_count, conv_weight, down_weight):
    regions = lax.axis_size("region")
    region = lax.axis_index("region")
    devices = lax.axis_size("chan")
    chan = lax.axis_index("chan")
    me = chan.reshape(1)
    slots = adjacency.shape[0]
    points = point_feats.shape[1]
    cells = slots * 512
    tiles = -(-(points // regions // LANES) // ID_ROWS)

    taps = conv_weight.transpose(2, 3, 0, 4, 1).reshape(9, conv_weight.shape[0], 192)
    down = down_weight.transpose(0, 2, 3, 4, 1).reshape(-1, conv_weight.shape[0], 128)
    mine = jnp.concatenate([taps, jnp.pad(down, ((0, 0), (0, 0), (0, 64)))], axis=0)
    theirs = [swap(mine, flip, devices) for flip in (1, 2, 3)]
    weights, down = prepare(me, mine, theirs, down_weight.shape[0])

    slot = voxel_slot // 512
    inside = voxel_slot % 512
    code = ((inside // 8) * slots + slot) * 8 + inside % 8
    keys, order = lax.sort(
        (destination * cells + code, jnp.arange(points, dtype=jnp.int32)), num_keys=1, is_stable=False
    )
    square = (points // LANES, LANES)
    moved = permute(point_feats, order.reshape(square), keys.reshape(square), theirs[-1], regions, cells)
    moved = lax.all_to_all(moved, "region", 0, 0, tiled=True)

    send_pos, hot = links(adjacency, region, regions, chan, devices)
    bounds = ranges(moved, tiles, slots)
    far = far_voxels(me, moved, bounds, slots, tiles)
    from_two = swap(far, 2, devices)
    near, faces = near_voxels(me, moved, bounds, far, send_pos, slots, tiles)
    from_three = swap(near[0], 3, devices)
    from_one = swap(near[1], 1, devices)
    remote = send_faces(faces, chan, regions, devices)
    coarse = convolve(me, active_count, near, (from_one, from_two, from_three), remote, hot, weights, down)
    back = [swap(coarse[flip], flip, devices) for flip in (1, 2, 3)]
    return finish(me, coarse, back, slots)


def solution(mesh):
    return jax.shard_map(
        body,
        mesh=mesh,
        in_specs=(
            P("chan", "region"),
            P("region"),
            P("region"),
            P("region", None),
            P("region"),
            P("chan", None, None, None, None),
            P(None, "chan", None, None, None),
        ),
        out_specs=P("region", "chan"),
        check_vma=False,
    )
```

time: 132 us -> 98.3 us (0.74)
  blocking collectives: 33.1 us -> 0 us
  waiting for transfers between devices: 3.88 us -> 23.9 us
  Pallas kernels: 47.3 us -> 38.5 us
  starting transfers between devices: 24.2 us -> 19.9 us
  other arithmetic: 14.2 us -> 10.7 us
  local copies, waits for them, and re-layouts: 7.14 us -> 3.85 us
    all_gather x2 -> x0, blocking collectives: 24.7 us -> none  [the longest x1 18 us: body(): down = lax.all_gather(down_weight, 'chan', axis=1, tiled=True)]
    all_to_all x1, waiting for transfers between devices: 3.86 us -> 15.3 us  [body(): moved = lax.all_to_all(moved, 'region', 0, 0, tiled=True)]
    all_to_all x2 -> x0, starting transfers between devices: 10.9 us -> none  [the longest x1 7.25 us: body(): lax.all_to_all((key % cells).reshape(regions, per // LANES, LANES), 'regi...]
    pallas_call x3 -> x4, Pallas kernels: 38.1 us -> 28.9 us  [the longest x1 12.4 us: permute(): pl.pallas_call(functools.partial(permute_kernel, depth, width, cells), ou...]
    ppermute x4 -> x13, waiting for transfers between devices: 0.01 us -> 8.59 us  [the longest x9 8.58 us: swap(): lax.ppermute(value, 'chan', [(source, source ^ flip) for source in range(...]
    all_to_all x1 -> x0, blocking collectives: 8.42 us -> none  [body(): coarse = lax.all_to_all(coarse, 'chan', 0, 0, tiled=True)]
    ppermute x4 -> x13, starting transfers between devices: 7.37 us -> 13.6 us  [the longest x9 8.08 us: swap(): lax.ppermute(value, 'chan', [(source, source ^ flip) for source in range(...]
    unnamed x17 -> x6, local copies, waits for them, and re-layouts: 6.22 us -> 0.02 us
  transfers between devices with their start and end apart: 7 -> 14, of which waited for: 1 -> 4; matrix products, arithmetic and copies ran while one was open for 5% -> 12% of each run, Pallas kernels for 17% -> 30%
where the time goes in v2:
time: 98.3 us; the launch traced here: 97.9 us
  Pallas kernels  38.5 us (39%)
  waiting for transfers between devices  23.9 us (24%)
  starting transfers between devices  19.9 us (20%)
  other arithmetic  10.7 us (11%)
  local copies, waits for them, and re-layouts  3.85 us (4%)
  between operations  1.04 us (1%)
    all_to_all x1, waiting for transfers between devices, body(): moved = lax.all_to_all(moved, 'region', 0, 0, tiled=True)  15.3 us
    pallas_call x1, Pallas kernels, permute(): pl.pallas_call(functools.partial(permute_kernel, depth, width, cells), ou...  12.4 us
    ppermute x9, waiting for transfers between devices, swap(): lax.ppermute(value, 'chan', [(source, source ^ flip) for source in range(...  8.58 us
    ppermute x9, starting transfers between devices, swap(): lax.ppermute(value, 'chan', [(source, source ^ flip) for source in range(...  8.08 us
    pallas_call x1, Pallas kernels, convolve(): pl.pallas_call(functools.partial(conv_kernel, slots), out_shape=jax.Shape...  7.69 us
    pallas_call x1, Pallas kernels, near_voxels(): pl.pallas_call(functools.partial(near_kernel, slots), out_shape=(jax.Shap...  6.99 us
    sort x1, other arithmetic, body(): lax.sort((destination * cells + code, jnp.arange(points, dtype=jnp.int32)...  6.45 us
    all_to_all x1, starting transfers between devices, body(): moved = lax.all_to_all(moved, 'region', 0, 0, tiled=True)  6.27 us
  transfers between devices with their start and end apart: 14, of which 4 were waited for; matrix products, arithmetic and copies ran while one was open for 12% of the time, Pallas kernels for 30%

profile of v2, /device:TPU:0, one launch (start us, length us, event | category | flops | bytes accessed | tf_op | source)
XLA Modules:
  0.0 97.9 jit_solution(6475250704846388520)
XLA Ops:
  0.0 0.0 copy-start
  0.0 1.0 %copy.24 = bf16[128,2,2,2,16]{4,3,2,1,0:T(2,128)(2,1)S(1)} copy(bf16[128,2,2,2,16]{0,3,2,1,4:T(2,128)(2,1)} %bitcast.66) | data formatting | bytes 65536 | tf_op jit(solution)/shard_map/reshape | solution.py:482
  1.1 0.2 reshape.79
  1.2 1.0 copy.19
  2.2 0.1 reshape.77
  2.4 2.5 %collective-permute-start = (bf16[17,16,192]{2,1,0:T(8,128)(2,1)S(1)}, bf16[17,16,192]{2,1,0:T(8,128)(2,1)S(1)}, u32[]{:S(2)}, u32[]{:S(2)}) collective-permute-start(bf16[17,16,192]{2,1,0:T(8,128)(2,1)S(1)} %fusion.8.own), channel_id=1, source_target_pairs={{0,3},{1,2},{2,1},{3,0},{4,7},{5,6},{6,5},{7,4},{8,11},{9,10},{10,... | collective-permute-start | bytes 313352 | tf_op jit(solution)/shard_map/ppermute | solution.py:467
  4.9 0.7 collective-permute-start.8
  5.5 0.0 collective-permute-start.9
  5.6 0.7 compare_select_fusion
  6.4 0.5 fusion.2
  6.9 0.4 convert_reduce_fusion
  7.2 1.0 %fusion.13 = s32[16384]{0:T(1024)S(1)} fusion(s32[16384]{0:T(1024)} %param.10, s32[16384]{0:T(1024)} %param.11), kind=kLoop, calls=%fused_computation.33 | loop fusion | flops 720896 | bytes 196608 | tf_op jit(solution)/shard_map/add | solution.py:491
  8.3 6.4 %sort.15 = (s32[16384]{0:T(1024)S(1)}, s32[16384]{0:T(1024)S(1)}) sort(s32[16384]{0:T(1024)S(1)} %fusion.13, s32[16384]{0:T(1024)S(1)} %iota.30), dimensions={0}, to_apply=%region_0.1 | sort | flops 229376 | bytes 262144 | tf_op jit(solution)/shard_map/sort | solution.py:490
  14.7 0.4 convert_reduce_fusion.1
  15.1 0.0 collective-permute-done.ready.three
  15.1 0.0 copy-done
  15.1 12.4 %permute.1 = bf16[8,18,16,128]{3,2,1,0:T(8,128)(2,1)} custom-call(bf16[16,16384]{1,0:T(8,128)(2,1)S(1)} %copy-done, s32[128,128]{1,0:T(8,128)S(1)} %bitcast.64, s32[128,128]{1,0:T(8,128)S(1)} %bitcast.63, bf16[17,16,192]{2,1,0:T(8,128)(2,1)S(1)} %collective-permute-done.ready.three), custom_call_target="tpu_custom_call" | custom-call | tf_op jit(solution)/shard_map/permute/pallas_call | solution.py:82
  27.5 6.3 %all-to-all-start = ((bf16[8,18,16,128]{3,2,1,0:T(8,128)(2,1)}), bf16[8,18,16,128]{3,2,1,0:T(8,128)(2,1)S(1)}, u32[]{:S(2)}, u32[]{:S(2)}) async-start(bf16[8,18,16,128]{3,2,1,0:T(8,128)(2,1)} %permute.1), calls=%async_computation | async-start | bytes 1179648 | tf_op jit(solution)/shard_map/all_to_all | solution.py:495
  33.8 0.2 concatenate.12
  34.0 0.1 convert_reduce_fusion.4
  34.2 15.3 %all-to-all-done.feats = bf16[8,18,16,128]{3,2,1,0:T(8,128)(2,1)S(1)} async-done(((bf16[8,18,16,128]{3,2,1,0:T(8,128)(2,1)}), bf16[8,18,16,128]{3,2,1,0:T(8,128)(2,1)S(1)}, u32[]{:S(2)}, u32[]{:S(2)}) %all-to-all-start) | async-done | bytes 589856 | tf_op jit(solution)/shard_map/all_to_all | solution.py:495
  49.5 0.7 slice.64
  50.3 0.4 slice_reduce_fusion
  50.7 0.7 convert_reduce_fusion.2
  51.3 0.1 subtract_reduce_fusion
  51.5 0.1 copy.23.hops
  51.5 6.2 %far_voxels.1.far = bf16[4,512,128]{2,1,0:T(8,128)(2,1)S(1)} custom-call(s32[1]{0:T(128)} %bitcast.chan, bf16[8,18,16,128]{3,2,1,0:T(8,128)(2,1)S(1)} %all-to-all-done.feats, s32[16,8]{1,0:T(8,128)S(1)} %get-tuple-element.44.first, s32[16,8]{1,0:T(8,128)S(1)} %get-tuple-element.43.last, s32[16,1]{1,0:T(8,128)S(1)} %copy.23.hops), custom_call_target="tpu_custom_call" | custom-call | flops 4000000000 | bytes 1200000 | tf_op jit(solution)/shard_map/far_voxels/pallas_call | solution.py:207
  57.7 2.3 %collective-permute-start.2 = (bf16[4,512,128]{2,1,0:T(8,128)(2,1)S(1)}, bf16[4,512,128]{2,1,0:T(8,128)(2,1)S(1)}, u32[]{:S(2)}, u32[]{:S(2)}) collective-permute-start(bf16[4,512,128]{2,1,0:T(8,128)(2,1)S(1)} %far_voxels.1.far), channel_id=1, source_target_pairs={{0,2},{1,3},{2,0},{3,1},{4,6},{5,7},{6,4},{7,5},{8,10},{9,11},{10,... | collective-permute-start | bytes 1572872 | tf_op jit(solution)/shard_map/ppermute | solution.py:467
  60.0 7.0 %near_voxels.1 = (bf16[3,4,512,128]{3,2,1,0:T(8,128)(2,1)S(1)}, bf16[2,8,16,128]{3,2,1,0:T(8,128)(2,1)S(1)}) custom-call(s32[1]{0:T(128)} %bitcast.chan, bf16[8,18,16,128]{3,2,1,0:T(8,128)(2,1)S(1)} %all-to-all-done.feats, s32[16,8]{1,0:T(8,128)S(1)} %get-tuple-element.44.first, s32[16,8]{1,0:T(8,128)S(1)} %get-tuple-element.43.last, ...), custom_call_target="tpu_custom_call" | custom-call | flops 4000000000 | bytes 3000000 | tf_op jit(solution)/shard_map/near_voxels/pallas_call | solution.py:223
  67.0 0.0 copy-start.1
  67.0 0.1 slice_bitcast_fusion
  67.1 0.1 collective-permute-start.1
  67.2 0.1 collective-permute-start.3
  67.3 0.0 collective-permute-done.8.one
  67.3 3.2 %collective-permute-start.4 = (bf16[8,16,128]{2,1,0:T(8,128)(2,1)S(1)}, bf16[8,16,128]{2,1,0:T(8,128)(2,1)S(1)}, u32[]{:S(2)}, u32[]{:S(2)}) collective-permute-start(bf16[8,16,128]{2,1,0:T(8,128)(2,1)S(1)} %get-tuple-element.30), channel_id=1, source_target_pairs={{0,4},{4,8},{8,12},{12,16},{16,20},{20,24},{24,28},{7,3},{11,7},{1... | collective-permute-start | bytes 98312 | tf_op jit(solution)/shard_map/ppermute | solution.py:462
  70.5 0.0 collective-permute-done.9.two
  70.5 0.7 collective-permute-start.5
  71.2 0.3 fusion.hot
  72.1 0.0 collective-permute-done.4.r0
  72.1 0.7 collective-permute-start.6
  72.8 0.0 collective-permute-done.5.r1
  72.8 0.0 copy-start.2
  72.8 1.0 %collective-permute-start.7 = (bf16[8,16,128]{2,1,0:T(8,128)(2,1)S(1)}, bf16[8,16,128]{2,1,0:T(8,128)(2,1)S(1)}, u32[]{:S(2)}, u32[]{:S(2)}) collective-permute-start(bf16[8,16,128]{2,1,0:T(8,128)(2,1)S(1)} %get-tuple-element.28), channel_id=1, source_target_pairs={{3,4},{7,8},{11,12},{15,16},{19,20},{23,24},{27,28},{4,3},{8,7},{1... | collective-permute-start | bytes 98312 | tf_op jit(solution)/shard_map/ppermute | solution.py:462
  73.9 0.0 copy-done.1
  73.9 3.4 %prepare.1 = (bf16[9,384,256]{2,1,0:T(8,128)(2,1)S(1)}, bf16[128,512]{1,0:T(8,128)(2,1)S(1)}) custom-call(s32[1]{0:T(128)} %bitcast.chan, bf16[4,384,192]{2,1,0:T(8,128)(2,1)S(1)} %copy-done.1, bf16[17,16,192]{2,1,0:T(8,128)(2,1)S(1)} %fusion.8.own, bf16[17,16,192]{2,1,0:T(8,128)(2,1)S(1)} %collective-permute-done.8.one, ...), custom_call_target="tpu_custom_call" | custom-call | flops 2000000000 | bytes 3000000 | tf_op jit(solution)/shard_map/prepare/pallas_call | solution.py:280
  77.3 0.0 collective-permute-done.6.r2
  77.3 0.0 collective-permute-done.7.r3
  77.3 0.0 collective-permute-done.1.one
  77.3 4.2 %collective-permute-done.3.three = bf16[4,512,128]{2,1,0:T(8,128)(2,1)S(1)} collective-permute-done((bf16[4,512,128]{2,1,0:T(8,128)(2,1)S(1)}, bf16[4,512,128]{2,1,0:T(8,128)(2,1)S(1)}, u32[]{:S(2)}, u32[]{:S(2)}) %collective-permute-start.3) | collective-permute-done | bytes 524320 | tf_op jit(solution)/shard_map/ppermute | solution.py:467
  81.5 0.0 collective-permute-done.2.two
  81.5 0.0 copy-done.2
  81.5 7.7 %convolve.1.own = bf16[4,32,1024]{2,1,0:T(8,128)(2,1)S(1)} custom-call(s32[1]{0:T(128)} %bitcast.chan, s32[1]{0:T(128)S(6)} %copy.26.active, bf16[3,4,512,128]{3,2,1,0:T(8,128)(2,1)S(1)} %get-tuple-element.13.near, bf16[4,512,128]{2,1,0:T(8,128)(2,1)S(1)} %collective-permute-done.1.one, bf16[4,512,128]{2,1,0:T(8,128)(2,1)S(1)} %collective-permute-done.2.two, ...), custom_call_target="tpu_custom_call" | custom-call | flops 6000000000 | bytes 5000000 | tf_op jit(solution)/shard_map/convolve/pallas_call | solution.py:381
  89.2 0.1 collective-permute-start.10
  89.3 2.4 %collective-permute-start.11 = (bf16[32,1024]{1,0:T(8,128)(2,1)S(1)}, bf16[32,1024]{1,0:T(8,128)(2,1)S(1)}, u32[]{:S(2)}, u32[]{:S(2)}) collective-permute-start(bf16[32,1024]{1,0:T(8,128)(2,1)S(1)} %get-tuple-element.26), channel_id=1, source_target_pairs={{0,2},{1,3},{2,0},{3,1},{4,6},{5,7},{6,4},{7,5},{8,10},{9,11},{10,... | collective-permute-start | bytes 196616 | tf_op jit(solution)/shard_map/ppermute | solution.py:467
  91.7 0.0 collective-permute-start.12
  91.7 0.0 collective-permute-done.10.one
  91.7 2.3 %collective-permute-done.11.two = bf16[32,1024]{1,0:T(8,128)(2,1)S(1)} collective-permute-done((bf16[32,1024]{1,0:T(8,128)(2,1)S(1)}, bf16[32,1024]{1,0:T(8,128)(2,1)S(1)}, u32[]{:S(2)}, u32[]{:S(2)}) %collective-permute-start.11) | collective-permute-done | bytes 65568 | tf_op jit(solution)/shard_map/ppermute | solution.py:467
  94.0 2.0 %collective-permute-done.12.three = bf16[32,1024]{1,0:T(8,128)(2,1)S(1)} collective-permute-done((bf16[32,1024]{1,0:T(8,128)(2,1)S(1)}, bf16[32,1024]{1,0:T(8,128)(2,1)S(1)}, u32[]{:S(2)}, u32[]{:S(2)}) %collective-permute-start.12) | collective-permute-done | bytes 65568 | tf_op jit(solution)/shard_map/ppermute | solution.py:467
  96.1 1.9 %finish.1 = bf16[64,2048]{1,0:T(8,128)(2,1)} custom-call(s32[1]{0:T(128)} %bitcast.chan, bf16[4,32,1024]{2,1,0:T(8,128)(2,1)S(1)} %convolve.1.own, bf16[32,1024]{1,0:T(8,128)(2,1)S(1)} %collective-permute-done.10.one, bf16[32,1024]{1,0:T(8,128)(2,1)S(1)} %collective-permute-done.11.two, bf16[32,1024]{1,0:T(8,128)(2,1)S(1)} %collective-permute-done.12.three), custom_call_target="tpu_custom_call" | custom-call | tf_op jit(solution)/shard_map/finish/pallas_call | solution.py:412
  (17 shorter events, 0.2 us)
Async XLA Ops:
  0.0 15.1 %copy-start = (bf16[16,16384]{1,0:T(8,128)(2,1)S(1)}, bf16[16,16384]{1,0:T(8,128)(2,1)}, u32[]{:S(2)}) copy-start(bf16[16,16384]{1,0:T(8,128)(2,1)} %feats.1) | copy-start | bytes 1572868
  2.4 12.7 %collective-permute-start = (bf16[17,16,192]{2,1,0:T(8,128)(2,1)S(1)}, bf16[17,16,192]{2,1,0:T(8,128)(2,1)S(1)}, u32[]{:S(2)}, u32[]{:S(2)}) collective-permute-start(bf16[17,16,192]{2,1,0:T(8,128)(2,1)S(1)} %fusion.8.own), channel_id=1, source_target_pairs={{0,3},{1,2},{2,1},{3,0},{4,7},{5,6},{6,5},{7,4},{8,11},{9,10},{10,... | collective-permute-start | bytes 313352 | tf_op jit(solution)/shard_map/ppermute | solution.py:467
  4.9 62.4 %collective-permute-start.8 = (bf16[17,16,192]{2,1,0:T(8,128)(2,1)S(1)}, bf16[17,16,192]{2,1,0:T(8,128)(2,1)S(1)}, u32[]{:S(2)}, u32[]{:S(2)}) collective-permute-start(bf16[17,16,192]{2,1,0:T(8,128)(2,1)S(1)} %fusion.8.own), channel_id=1, source_target_pairs={{0,1},{1,0},{2,3},{3,2},{4,5},{5,4},{6,7},{7,6},{8,9},{9,8},{10,11... | collective-permute-start | bytes 313352 | tf_op jit(solution)/shard_map/ppermute | solution.py:467
  5.5 65.0 %collective-permute-start.9 = (bf16[17,16,192]{2,1,0:T(8,128)(2,1)S(1)}, bf16[17,16,192]{2,1,0:T(8,128)(2,1)S(1)}, u32[]{:S(2)}, u32[]{:S(2)}) collective-permute-start(bf16[17,16,192]{2,1,0:T(8,128)(2,1)S(1)} %fusion.8.own), channel_id=1, source_target_pairs={{0,2},{1,3},{2,0},{3,1},{4,6},{5,7},{6,4},{7,5},{8,10},{9,11},{10,... | collective-permute-start | bytes 313352 | tf_op jit(solution)/shard_map/ppermute | solution.py:467
  27.5 22.0 %all-to-all-start = ((bf16[8,18,16,128]{3,2,1,0:T(8,128)(2,1)}), bf16[8,18,16,128]{3,2,1,0:T(8,128)(2,1)S(1)}, u32[]{:S(2)}, u32[]{:S(2)}) async-start(bf16[8,18,16,128]{3,2,1,0:T(8,128)(2,1)} %permute.1), calls=%async_computation | async-start | bytes 1179648 | tf_op jit(solution)/shard_map/all_to_all | solution.py:495
  57.7 23.8 %collective-permute-start.2 = (bf16[4,512,128]{2,1,0:T(8,128)(2,1)S(1)}, bf16[4,512,128]{2,1,0:T(8,128)(2,1)S(1)}, u32[]{:S(2)}, u32[]{:S(2)}) collective-permute-start(bf16[4,512,128]{2,1,0:T(8,128)(2,1)S(1)} %far_voxels.1.far), channel_id=1, source_target_pairs={{0,2},{1,3},{2,0},{3,1},{4,6},{5,7},{6,4},{7,5},{8,10},{9,11},{10,... | collective-permute-start | bytes 1572872 | tf_op jit(solution)/shard_map/ppermute | solution.py:467
  67.0 6.9 %copy-start.1 = (bf16[4,384,192]{2,1,0:T(8,128)(2,1)S(1)}, bf16[4,384,192]{2,1,0:T(8,128)(2,1)}, u32[]{:S(2)}) copy-start(bf16[4,384,192]{2,1,0:T(8,128)(2,1)} %constant.111.clone.spread) | copy-start | bytes 1769476
  67.1 10.2 %collective-permute-start.1 = (bf16[4,512,128]{2,1,0:T(8,128)(2,1)S(1)}, bf16[4,512,128]{2,1,0:T(8,128)(2,1)S(1)}, u32[]{:S(2)}, u32[]{:S(2)}) collective-permute-start(bf16[4,512,128]{2,1,0:T(8,128)(2,1)S(1)} %get-tuple-element.24), channel_id=1, source_target_pairs={{0,1},{1,0},{2,3},{3,2},{4,5},{5,4},{6,7},{7,6},{8,9},{9,8},{10,11... | collective-permute-start | bytes 1572872 | tf_op jit(solution)/shard_map/ppermute | solution.py:467
  67.2 14.3 %collective-permute-start.3 = (bf16[4,512,128]{2,1,0:T(8,128)(2,1)S(1)}, bf16[4,512,128]{2,1,0:T(8,128)(2,1)S(1)}, u32[]{:S(2)}, u32[]{:S(2)}) collective-permute-start(bf16[4,512,128]{2,1,0:T(8,128)(2,1)S(1)} %get-tuple-element.23), channel_id=1, source_target_pairs={{0,3},{1,2},{2,1},{3,0},{4,7},{5,6},{6,5},{7,4},{8,11},{9,10},{10,... | collective-permute-start | bytes 1572872 | tf_op jit(solution)/shard_map/ppermute | solution.py:467
  67.3 4.8 %collective-permute-start.4 = (bf16[8,16,128]{2,1,0:T(8,128)(2,1)S(1)}, bf16[8,16,128]{2,1,0:T(8,128)(2,1)S(1)}, u32[]{:S(2)}, u32[]{:S(2)}) collective-permute-start(bf16[8,16,128]{2,1,0:T(8,128)(2,1)S(1)} %get-tuple-element.30), channel_id=1, source_target_pairs={{0,4},{4,8},{8,12},{12,16},{16,20},{20,24},{24,28},{7,3},{11,7},{1... | collective-permute-start | bytes 98312 | tf_op jit(solution)/shard_map/ppermute | solution.py:462
  70.5 2.3 %collective-permute-start.5 = (bf16[8,16,128]{2,1,0:T(8,128)(2,1)S(1)}, bf16[8,16,128]{2,1,0:T(8,128)(2,1)S(1)}, u32[]{:S(2)}, u32[]{:S(2)}) collective-permute-start(bf16[8,16,128]{2,1,0:T(8,128)(2,1)S(1)} %get-tuple-element.31), channel_id=1, source_target_pairs={{1,4},{5,8},{9,12},{13,16},{17,20},{21,24},{25,28},{6,3},{10,7},{1... | collective-permute-start | bytes 98312 | tf_op jit(solution)/shard_map/ppermute | solution.py:462
  72.1 5.1 %collective-permute-start.6 = (bf16[8,16,128]{2,1,0:T(8,128)(2,1)S(1)}, bf16[8,16,128]{2,1,0:T(8,128)(2,1)S(1)}, u32[]{:S(2)}, u32[]{:S(2)}) collective-permute-start(bf16[8,16,128]{2,1,0:T(8,128)(2,1)S(1)} %get-tuple-element.29), channel_id=1, source_target_pairs={{2,4},{6,8},{10,12},{14,16},{18,20},{22,24},{26,28},{5,3},{9,7},{1... | collective-permute-start | bytes 98312 | tf_op jit(solution)/shard_map/ppermute | solution.py:462
  72.8 8.7 %copy-start.2 = (bf16[512,256]{1,0:T(8,128)(2,1)S(1)}, bf16[512,256]{1,0:T(8,128)(2,1)}, u32[]{:S(2)}) copy-start(bf16[512,256]{1,0:T(8,128)(2,1)} %constant.112.clone.pick) | copy-start | bytes 786436
  72.8 4.5 %collective-permute-start.7 = (bf16[8,16,128]{2,1,0:T(8,128)(2,1)S(1)}, bf16[8,16,128]{2,1,0:T(8,128)(2,1)S(1)}, u32[]{:S(2)}, u32[]{:S(2)}) collective-permute-start(bf16[8,16,128]{2,1,0:T(8,128)(2,1)S(1)} %get-tuple-element.28), channel_id=1, source_target_pairs={{3,4},{7,8},{11,12},{15,16},{19,20},{23,24},{27,28},{4,3},{8,7},{1... | collective-permute-start | bytes 98312 | tf_op jit(solution)/shard_map/ppermute | solution.py:462
  89.2 2.5 %collective-permute-start.10 = (bf16[32,1024]{1,0:T(8,128)(2,1)S(1)}, bf16[32,1024]{1,0:T(8,128)(2,1)S(1)}, u32[]{:S(2)}, u32[]{:S(2)}) collective-permute-start(bf16[32,1024]{1,0:T(8,128)(2,1)S(1)} %get-tuple-element.27), channel_id=1, source_target_pairs={{0,1},{1,0},{2,3},{3,2},{4,5},{5,4},{6,7},{7,6},{8,9},{9,8},{10,11... | collective-permute-start | bytes 196616 | tf_op jit(solution)/shard_map/ppermute | solution.py:467
  89.3 4.7 %collective-permute-start.11 = (bf16[32,1024]{1,0:T(8,128)(2,1)S(1)}, bf16[32,1024]{1,0:T(8,128)(2,1)S(1)}, u32[]{:S(2)}, u32[]{:S(2)}) collective-permute-start(bf16[32,1024]{1,0:T(8,128)(2,1)S(1)} %get-tuple-element.26), channel_id=1, source_target_pairs={{0,2},{1,3},{2,0},{3,1},{4,6},{5,7},{6,4},{7,5},{8,10},{9,11},{10,... | collective-permute-start | bytes 196616 | tf_op jit(solution)/shard_map/ppermute | solution.py:467
  91.7 4.4 %collective-permute-start.12 = (bf16[32,1024]{1,0:T(8,128)(2,1)S(1)}, bf16[32,1024]{1,0:T(8,128)(2,1)S(1)}, u32[]{:S(2)}, u32[]{:S(2)}) collective-permute-start(bf16[32,1024]{1,0:T(8,128)(2,1)S(1)} %get-tuple-element.25), channel_id=1, source_target_pairs={{0,3},{1,2},{2,1},{3,0},{4,7},{5,6},{6,5},{7,4},{8,11},{9,10},{10,... | collective-permute-start | bytes 196616 | tf_op jit(solution)/shard_map/ppermute | solution.py:467

commit v3 on v2

v3 whole, which is shorter than its diff:
```python
import functools

import jax
import jax.numpy as jnp
import numpy as np
from jax import lax
from jax.experimental import pallas as pl
from jax.experimental.pallas import tpu as pltpu
from jax.sharding import PartitionSpec as P

OFFSETS = [
    (first, second, third)
    for first in (-1, 0, 1)
    for second in (-1, 0, 1)
    for third in (-1, 0, 1)
    if (first, second, third) != (0, 0, 0)
]
LANES = 128
REACH = 16
F32 = jnp.float32
BF16 = jnp.bfloat16
NT = (((1,), (1,)), ((), ()))
VMEM = pl.BlockSpec(memory_space=pltpu.VMEM)
SMEM = pl.BlockSpec(memory_space=pltpu.SMEM)


def mm(a, b):
    return jnp.dot(a, b, preferred_element_type=F32)


def params():
    return pltpu.CompilerParams(vmem_limit_bytes=24 * 1024 * 1024)


ID_ROWS = 16
GROUP = 8


def one_hot_columns(depth, stack, wanted, channels=16):
    count = wanted.shape[0]
    width = count * LANES
    wanted = jnp.concatenate([wanted[i : i + 1] for i in range(count)], axis=1)
    low = (wanted & (depth - 1)).astype(jnp.int16)
    top = wanted // depth
    hot = lax.broadcasted_iota(jnp.int16, (depth, width), 0) == low
    hot = jnp.where(hot, jnp.ones((), BF16), jnp.zeros((), BF16))
    found = mm(stack[...], hot)
    picked = jnp.zeros((channels, width), F32)
    for part in range(stack.shape[0] // channels):
        picked = jnp.where(top == part, found[part * channels : (part + 1) * channels], picked)
    return picked.astype(BF16)


def fill_stack(depth, feats, stack):
    channels, points = feats.shape
    for part in range(points // depth):
        stack[part * channels : (part + 1) * channels, :] = feats[:, part * depth : (part + 1) * depth]


def put_codes(out, blocks, tiles, tile, rows):
    if rows.shape[0] < ID_ROWS:
        rows = jnp.concatenate([rows, jnp.zeros((ID_ROWS - rows.shape[0], LANES), jnp.int32)], axis=0)
    out[blocks + tile] = (rows >> 8).astype(F32).astype(BF16)
    out[blocks + tiles + tile] = (rows & 255).astype(F32).astype(BF16)


def permute_kernel(depth, width, cells, feats, order, keys, out, stack):
    channels, points = feats.shape
    fill_stack(depth, feats, stack)
    regions = out.shape[0]
    blocks = points // regions // LANES
    tiles = (out.shape[1] - blocks) // 2
    count = width // LANES

    def step(at, _):
        picked = one_hot_columns(depth, stack, order[pl.ds(at * count, count), :])
        for part in range(count):
            tile = at * count + part
            out[tile // blocks, tile % blocks] = picked[:, part * LANES : (part + 1) * LANES]
        return 0

    lax.fori_loop(0, points // width, step, 0)
    for target in range(regions):
        for tile in range(tiles):
            begin = target * blocks + tile * ID_ROWS
            rows = min(ID_ROWS, blocks - tile * ID_ROWS)
            put_codes(out.at[target], blocks, tiles, tile, lax.rem(keys[begin : begin + rows, :], cells))


def permute(feats, order, keys, regions, cells):
    channels, points = feats.shape
    depth, width = 512, 1024
    blocks = points // regions // LANES
    tiles = -(-blocks // ID_ROWS)
    return pl.pallas_call(
        functools.partial(permute_kernel, depth, width, cells),
        out_shape=jax.ShapeDtypeStruct((regions, blocks + 2 * tiles, channels, LANES), BF16),
        in_specs=[VMEM] * 3,
        out_specs=VMEM,
        scratch_shapes=[pltpu.VMEM((points // depth * channels, depth), BF16)],
        compiler_params=params(),
        name="permute",
    )(feats, order, keys)


def piece_kernel(depth, cells, flips, region, feats, order, keys, *rest):
    outs = rest[-1 - len(flips) : -1]
    stack = rest[-1]
    fill_stack(depth, feats, stack)
    tiles = 1
    blocks = outs[0].shape[0] - 2 * tiles
    count = 8
    for flip, out in zip(flips, outs):
        begin = pl.multiple_of((region[0] ^ flip) * blocks, 8)
        for step in range(blocks // count):
            picked = one_hot_columns(depth, stack, order[pl.ds(begin + step * count, count), :])
            for part in range(count):
                out[step * count + part] = picked[:, part * LANES : (part + 1) * LANES]
        put_codes(out, blocks, tiles, 0, lax.rem(keys[pl.ds(begin, blocks), :], cells))


def permute_piece(flips, region, feats, order, keys, regions, cells, before=()):
    channels, points = feats.shape
    depth = 512
    blocks = points // regions // LANES
    return pl.pallas_call(
        functools.partial(piece_kernel, depth, cells, flips),
        out_shape=[jax.ShapeDtypeStruct((blocks + 2, channels, LANES), BF16)] * len(flips),
        in_specs=[SMEM] + [VMEM] * 3 + [pl.BlockSpec(memory_space=pl.ANY)] * len(before),
        out_specs=[VMEM] * len(flips),
        scratch_shapes=[pltpu.VMEM((points // depth * channels, depth), BF16)],
        compiler_params=params(),
        cost_estimate=pl.CostEstimate(flops=2_000_000_000, bytes_accessed=1_000_000, transcendentals=0),
        name="permute_piece",
    )(region, feats, order, keys, *before)


def exchange(feats, order, keys, region, regions, cells):
    blocks = feats.shape[1] // regions // LANES
    if regions != GROUP or blocks != ID_ROWS:
        moved = permute(feats, order, keys, regions, cells)
        return [lax.all_to_all(moved, "region", 0, 0, tiled=True)], moved

    def send(values, flips):
        pairs = [[(source, source ^ flip) for source in range(regions)] for flip in flips]
        return [lax.ppermute(value, "region", pair) for value, pair in zip(values, pairs)]

    at = region.reshape(1)
    made = []
    got = []
    for number, flips in enumerate(((6, 7), (4, 5), (2, 3), (1, 0))):
        before = got[number - 2] if number >= 2 else ()
        values = permute_piece(flips, at, feats, order, keys, regions, cells, before)
        made.append(values)
        if number < 3:
            got.append(send(values, flips))
        else:
            got.append(send(values[:1], flips[:1]) + list(values[1:]))
    return [chunk for some in got for chunk in some], made[1][0]


WINDOW = 256
STATIC = 2


def chunk_of(chunks, number):
    return chunks[0].at[number] if len(chunks) == 1 else chunks[number]


def decode(chunks, ids, ends, places):
    count, padded_blocks, _ = ids.shape
    tiles = padded_blocks // ID_ROWS
    blocks = chunk_of(chunks, 0).shape[0] - 2 * tiles
    bounds = lax.broadcasted_iota(jnp.int32, (ID_ROWS, LANES), 1) * (WINDOW * 8)
    row = lax.broadcasted_iota(jnp.int32, (ID_ROWS, LANES), 0)
    for chunk in range(count):
        first = jnp.zeros((1, LANES), jnp.int32)
        last = jnp.zeros((1, LANES), jnp.int32)
        for tile in range(tiles):
            upper = chunk_of(chunks, chunk)[blocks + tile].astype(F32)
            lower = chunk_of(chunks, chunk)[blocks + tiles + tile].astype(F32)
            code = (upper * 256.0 + lower).astype(jnp.int32)
            ids[chunk, tile * ID_ROWS : (tile + 1) * ID_ROWS, :] = code
            real = row + tile * ID_ROWS < blocks
            passed = real & (code[:, LANES - 1 :] < bounds)
            begun = real & (code[:, 0:1] < bounds + WINDOW * 8)
            first += jnp.sum(jnp.where(passed, 1, 0), axis=0, keepdims=True)
            last += jnp.sum(jnp.where(begun, 1, 0), axis=0, keepdims=True)
        ends[chunk : chunk + 1, :] = first
        ends[count + chunk : count + chunk + 1, :] = last
    pltpu.sync_copy(ends, places)


def window_mean(number, chunks, ids, places, acc):
    count, padded_blocks, _ = ids.shape
    channels = chunk_of(chunks, 0).shape[1]
    groups = count // GROUP
    blocks = chunk_of(chunks, 0).shape[0] - 2 * (padded_blocks // ID_ROWS)

    def product(group, steps):
        sides = []
        rows = []
        for at in steps:
            for member in range(GROUP):
                chunk = group * GROUP + member
                block = places[chunk, number] + at
                valid = block < places[count + chunk, number]
                block = jnp.minimum(block, blocks - 1)
                code = ids[chunk, pl.ds(block, 1), :]
                cell = code & 7
                rows.append(jnp.where(valid, (code >> 3) - number * WINDOW, -1))
                values = chunk_of(chunks, chunk)[block].astype(F32)
                mask = [cell == k for k in range(8)]
                side = [jnp.where(m, values, 0.0).astype(BF16) for m in mask]
                side += [jnp.broadcast_to(jnp.where(m, 1.0, 0.0), (channels, LANES)).astype(BF16) for m in mask]
                sides.append(jnp.concatenate(side, axis=0))
        side = jnp.concatenate(sides, axis=1)
        row = jnp.concatenate(rows, axis=1).astype(jnp.int16)
        hot = lax.broadcasted_iota(jnp.int16, (WINDOW, len(steps) * GROUP * LANES), 0) == row
        hot = jnp.where(hot, jnp.ones((), BF16), jnp.zeros((), BF16))
        return lax.dot_general(hot, side, NT, preferred_element_type=F32)

    def one_group(group, start):
        def step(at, _):
            acc[...] += product(group, [at])
            return 0

        hops = 0
        for member in range(GROUP):
            chunk = group * GROUP + member
            hops = jnp.maximum(hops, places[count + chunk, number] - places[chunk, number])
        lax.fori_loop(start, hops, step, 0)

    if groups == 1:
        acc[...] = product(0, list(range(STATIC)))
        one_group(0, STATIC)
    else:
        acc[...] = jnp.zeros_like(acc)

        def each(group, _):
            one_group(group, 0)
            return 0

        lax.fori_loop(0, groups, each, 0)
    return (acc[:, :LANES] / jnp.maximum(acc[:, LANES:], 1.0)).astype(BF16)


def far_kernel(count, chan, *rest):
    chunks = rest[:count]
    out, ids, acc, ends, places = rest[-5:]
    decode(chunks, ids, ends, places)
    begin = 2 * (chan[0] ^ 2) + 7
    parts = out.shape[1] // WINDOW
    for plane in range(out.shape[0]):
        for part in range(parts):
            number = lax.rem(begin + plane, 8) * parts + part
            out[plane, part * WINDOW : (part + 1) * WINDOW, :] = window_mean(number, chunks, ids, places, acc)


def near_kernel(slots, count, chan, *rest):
    chunks = rest[:count]
    far, send_pos, three, one, own, f0, f1, f2, f3, ids, acc, ends, places, planes = rest[count:]
    decode(chunks, ids, ends, places)
    partner = chan[0] ^ 2
    begin = 2 * partner + 7
    parts = far.shape[1] // WINDOW
    planes[0:4] = far[...]
    for plane in range(4, 8):
        for part in range(parts):
            number = lax.rem(begin + plane, 8) * parts + part
            planes[plane, part * WINDOW : (part + 1) * WINDOW, :] = window_mean(number, chunks, ids, places, acc)
    for out, flip in ((three, 3), (one, 1), (own, 0)):
        shift = 2 * ((chan[0] ^ flip) - partner) + 8
        for plane in range(4):
            out[plane] = planes[lax.rem(shift + plane, 8)]
    compact = []
    for side in range(2):
        hot = lax.broadcasted_iota(jnp.int32, (REACH, slots), 0) == send_pos[side : side + 1, :]
        compact.append(jnp.where(hot, 1.0, 0.0).astype(BF16))
    last_plane, first_plane = (planes.at[lax.rem(at - begin + 16, 8)] for at in (7, 8))
    for j in range(8):
        rows = slice(j * slots, (j + 1) * slots)
        to_next = mm(compact[0], last_plane[rows, :])
        to_previous = mm(compact[1], first_plane[rows, :])
        for flip, out in enumerate((f0, f1, f2, f3)):
            out[j] = jnp.where(chan[0] == flip, to_next, to_previous).astype(BF16)


def voxel_scratch(chunks, regions):
    total = chunks[0].shape[-3]
    tiles = -(-total // (ID_ROWS + 2))
    return [
        pltpu.VMEM((regions, tiles * ID_ROWS, LANES), jnp.int32),
        pltpu.VMEM((WINDOW, 2 * LANES), F32),
        pltpu.VMEM((2 * regions, LANES), jnp.int32),
        pltpu.SMEM((2 * regions, LANES), jnp.int32),
    ]


def far_voxels(chan, chunks, regions, slots, before):
    return pl.pallas_call(
        functools.partial(far_kernel, len(chunks)),
        out_shape=jax.ShapeDtypeStruct((4, 8 * slots, LANES), BF16),
        in_specs=[SMEM] + [VMEM] * len(chunks) + [pl.BlockSpec(memory_space=pl.ANY)] * len(before),
        out_specs=VMEM,
        scratch_shapes=voxel_scratch(chunks, regions),
        compiler_params=params(),
        cost_estimate=pl.CostEstimate(flops=4_000_000_000, bytes_accessed=1_200_000, transcendentals=0),
        name="far_voxels",
    )(chan, *chunks, *before)


def near_voxels(chan, chunks, regions, far, send_pos, slots):
    return pl.pallas_call(
        functools.partial(near_kernel, slots, len(chunks)),
        out_shape=[jax.ShapeDtypeStruct((4, 8 * slots, LANES), BF16)] * 3
        + [jax.ShapeDtypeStruct((8, REACH, LANES), BF16)] * 4,
        in_specs=[SMEM] + [VMEM] * len(chunks) + [VMEM, VMEM],
        out_specs=[VMEM] * 7,
        scratch_shapes=voxel_scratch(chunks, regions) + [pltpu.VMEM((8, 8 * slots, LANES), BF16)],
        compiler_params=params(),
        cost_estimate=pl.CostEstimate(flops=4_000_000_000, bytes_accessed=3_000_000, transcendentals=0),
        name="near_voxels",
    )(chan, *chunks, far, send_pos)


def spread_matrix():
    spread = np.zeros((4, 384, 192), np.float32)
    for k in range(4):
        for e in range(3):
            cell = k + e
            for channel in range(64):
                source, inner = divmod(channel, 16)
                if 1 <= cell <= 4:
                    row = source * 64 + (cell - 1) * 16 + inner
                else:
                    row = 256 + (cell // 5) * 64 + source * 16 + inner
                spread[k, row, e * 64 + channel] = 1
    return spread


def pack_kernel(conv, down, _, pack):
    for ab in range(9):
        for e in range(3):
            pack[ab, :, e * 64 : (e + 1) * 64] = conv[ab * 3 + e]
    for part in range(8):
        pack[9 + part, :, 0:128] = down[part * 16 : (part + 1) * 16, :]
        pack[9 + part, :, 128:192] = jnp.zeros((16, 64), BF16)


def pack(conv, down, before):
    return pl.pallas_call(
        pack_kernel,
        out_shape=jax.ShapeDtypeStruct((17, 16, 192), BF16),
        in_specs=[VMEM, VMEM, pl.BlockSpec(memory_space=pl.ANY)],
        out_specs=VMEM,
        compiler_params=params(),
        name="pack",
    )(conv, down, before)


def weight_kernel(chan, spread, own, one, two, three, even, odd, down):
    every = (own, one, two, three)
    columns = lax.broadcasted_iota(jnp.int32, (192, 192), 1) ^ (chan[0] * 16)
    turn = jnp.where(lax.broadcasted_iota(jnp.int32, (192, 192), 0) == columns, 1.0, 0.0).astype(BF16)
    for ab in range(9):
        taps = jnp.concatenate([ref[ab] for ref in every], axis=0)
        taps = mm(taps, turn).astype(BF16)
        for k in range(4):
            column = slice(k * 64, (k + 1) * 64)
            band = lax.dot_general(spread[k], taps, NT, preferred_element_type=F32).astype(BF16)
            for out, pair in ((even, (0, 2)), (odd, (1, 3))):
                for place, source in enumerate(pair):
                    main = band[source * 64 : source * 64 + 64]
                    out[0, ab, place * 64 : place * 64 + 64, column] = main
                    out[1, ab, 128 + place * 64 : 192 + place * 64, column] = main
                    for end in range(2):
                        edge = band[256 + end * 64 + source * 16 : 272 + end * 64 + source * 16]
                        row = end * 32 + place * 16
                        out[0, ab, 128 + row : 144 + row, column] = edge
                        out[1, ab, 64 + row : 80 + row, column] = edge
        for out in (even, odd):
            out[0, ab, 192:256, :] = jnp.zeros((64, 256), BF16)
            out[1, ab, 0:64, :] = jnp.zeros((64, 256), BF16)
    outputs = down.shape[0]
    total = jnp.zeros((outputs, 512), F32)
    rows = lax.broadcasted_iota(jnp.int32, (128, 512), 0)
    place = (rows & 7) * 64 + (rows >> 3)
    for source, ref in enumerate(every):
        part = ref[9:, :, 0:128].reshape(128, outputs)
        move = lax.broadcasted_iota(jnp.int32, (128, 512), 1) == place + source * 16
        move = jnp.where(move, 1.0, 0.0).astype(BF16)
        total += lax.dot_general(part, move, (((0,), (0,)), ((), ())), preferred_element_type=F32)
    down[...] = total.astype(BF16)


def prepare(chan, own, others, outputs):
    return pl.pallas_call(
        weight_kernel,
        out_shape=(
            jax.ShapeDtypeStruct((2, 9, 256, 256), BF16),
            jax.ShapeDtypeStruct((2, 9, 256, 256), BF16),
            jax.ShapeDtypeStruct((outputs, 512), BF16),
        ),
        in_specs=[SMEM] + [VMEM] * 5,
        out_specs=(VMEM, VMEM, VMEM),
        compiler_params=params(),
        cost_estimate=pl.CostEstimate(flops=2_000_000_000, bytes_accessed=3_000_000, transcendentals=0),
        name="prepare",
    )(chan, jnp.asarray(spread_matrix(), BF16), own, *others)


def halo_matrix():
    pick = np.zeros((256, 128), np.float32)
    for group, cell in enumerate((7, 4, 3, 0)):
        for source in range(2):
            for inner in range(16):
                pick[source * 128 + cell * 16 + inner, group * 32 + source * 16 + inner] = 1
    return pick


def pad_planes(slots, grid, remote, hot, pick, table, padded):
    total = slots + REACH
    lane = lax.broadcasted_iota(jnp.int32, (slots, LANES), 1)
    for plane in range(4):
        edge = mm(jnp.concatenate([ref[plane] for ref in grid], axis=1), pick[...]).astype(BF16)
        for j in range(8):
            rows = slice(j * slots, (j + 1) * slots)
            parts = [ref[plane, rows, :] for ref in grid]
            table[plane, j, 0:slots, 0:128] = jnp.concatenate([part[:, 0:64] for part in parts], axis=1)
            table[plane, j, 0:slots, 128:256] = edge[rows]
            table[plane, j, 0:slots, 256:384] = jnp.concatenate([part[:, 64:128] for part in parts], axis=1)
    for plane in (0, 3):
        for j in range(8):
            parts = [ref[j] for ref in remote]
            table[plane, j, slots:total, 0:128] = jnp.concatenate([part[:, 0:64] for part in parts], axis=1)
            table[plane, j, slots:total, 128:256] = mm(jnp.concatenate(parts, axis=1), pick[...]).astype(BF16)
            table[plane, j, slots:total, 256:384] = jnp.concatenate([part[:, 64:128] for part in parts], axis=1)

    for plane in range(4):
        base = (0, 9, 9, 18)[plane]
        used = total if plane in (0, 3) else slots
        for jj in range(10):
            dy, j = ((-1, 7) if jj == 0 else (1, 0) if jj == 9 else (0, jj - 1))
            at = base + (dy + 1) * 3
            source = table[plane, j, 0:used, :]
            if plane in (1, 2) and dy == 0:
                own = source
            else:
                own = mm(hot[at + 1, :, 0:used], source).astype(BF16)
            below = mm(hot[at, :, 0:used], source[:, 128:256]).astype(BF16)
            above = mm(hot[at + 2, :, 0:used], source[:, 128:256]).astype(BF16)
            padded[plane, jj, :, 0:128] = own[:, 0:128]
            padded[plane, jj, :, 128:256] = jnp.where(lane < 32, below, jnp.where(lane < 96, own[:, 128:256], above))
            padded[plane, jj, :, 256:384] = own[:, 256:384]


def products(padded, weights, half, a_out, start):
    slots = padded.shape[2]
    for ab in range(9):
        left = padded[a_out + ab // 3, ab % 3 : ab % 3 + 8, :, half * 128 : half * 128 + 256]
        term = mm(left.reshape(8 * slots, 256), weights[half, ab])
        start = term if start is None else start + term
    return start


def even_kernel(slots, own, two, r0, r2, hot, pick, weights, sums, table, padded):
    pad_planes(slots, (own, two), (r0, r2), hot, pick, table, padded)
    for half in range(2):
        for a_out in range(2):
            sums[half, a_out] = products(padded, weights, half, a_out, None)


def odd_kernel(slots, chan, active, one, three, r1, r3, hot, pick, weights, down, sums, *rest):
    table, padded, stacked, answer = rest[4:]
    pad_planes(slots, (one, three), (r1, r3), hot, pick, table, padded)
    alive = lax.broadcasted_iota(jnp.int32, (slots, 256), 0) < active[0]
    for half in range(2):
        for a_out in range(2):
            total_sum = products(padded, weights, half, a_out, sums[half, a_out])
            for j in range(8):
                block = jnp.where(alive, jnp.maximum(total_sum[j * slots : (j + 1) * slots], 0.0), 0.0).astype(BF16)
                for kk in range(2):
                    begin = ((j // 2) * 4 + half * 2 + kk) * slots
                    place = (a_out * 2 + j % 2) * 128
                    stacked[begin : begin + slots, place : place + 128] = block[:, kk * 128 : kk * 128 + 128]

    result = lax.dot_general(down[...], stacked[...], NT, preferred_element_type=F32)
    answer[...] = jnp.maximum(result, 0.0).astype(BF16)
    width = rest[0].shape[0]
    for flip in range(4):
        rest[flip][...] = answer[pl.ds(pl.multiple_of((chan[0] ^ flip) * width, width), width), :]


def even_sums(own, two, remote, hot, weights):
    slots = own.shape[1] // 8
    return pl.pallas_call(
        functools.partial(even_kernel, slots),
        out_shape=jax.ShapeDtypeStruct((2, 2, 8 * slots, 256), F32),
        in_specs=[VMEM] * 7,
        out_specs=VMEM,
        scratch_shapes=[
            pltpu.VMEM((4, 8, slots + REACH, 384), BF16),
            pltpu.VMEM((4, 10, slots, 384), BF16),
        ],
        compiler_params=params(),
        cost_estimate=pl.CostEstimate(flops=4_000_000_000, bytes_accessed=5_000_000, transcendentals=0),
        name="even_sums",
    )(own, two, *remote, hot, jnp.asarray(halo_matrix(), BF16), weights)


def convolve(chan, active, one, three, remote, hot, weights, down, sums):
    devices = 4
    slots = one.shape[1] // 8
    outputs = down.shape[0]
    return pl.pallas_call(
        functools.partial(odd_kernel, slots),
        out_shape=[jax.ShapeDtypeStruct((outputs // devices, 16 * slots), BF16)] * devices,
        in_specs=[SMEM] * 2 + [VMEM] * 9,
        out_specs=[VMEM] * devices,
        scratch_shapes=[
            pltpu.VMEM((4, 8, slots + REACH, 384), BF16),
            pltpu.VMEM((4, 10, slots, 384), BF16),
            pltpu.VMEM((16 * slots, 512), BF16),
            pltpu.VMEM((outputs, 16 * slots), BF16),
        ],
        compiler_params=params(),
        cost_estimate=pl.CostEstimate(flops=4_000_000_000, bytes_accessed=5_000_000, transcendentals=0),
        name="convolve",
    )(chan, active, one, three, *remote, hot, jnp.asarray(halo_matrix(), BF16), weights, down, sums)


def final_kernel(slots, chan, own, one, two, three, out, turned):
    outputs = own.shape[0]
    for flip, ref in enumerate((own, one, two, three)):
        plane = chan[0] ^ flip
        for cell in range(16):
            turned[pl.ds(plane * 16 + cell, outputs, stride=64), :] = ref[
                :, cell * slots : (cell + 1) * slots
            ].astype(F32)
    for tile in range(out.shape[1] // LANES):
        out[:, tile * LANES : (tile + 1) * LANES] = turned[tile * LANES : (tile + 1) * LANES, :].T.astype(BF16)


def finish(chan, coarse, others, slots):
    outputs = coarse.shape[0]
    return pl.pallas_call(
        functools.partial(final_kernel, slots),
        out_shape=jax.ShapeDtypeStruct((slots, outputs * 64), BF16),
        in_specs=[SMEM] + [VMEM] * 4,
        out_specs=VMEM,
        scratch_shapes=[pltpu.VMEM((outputs * 64, slots), F32)],
        compiler_params=params(),
        name="finish",
    )(chan, coarse, *others)


def links(adjacency, region, regions, chan, devices):
    slots = adjacency.shape[0]
    named = adjacency.T
    linked = named < slots * regions
    owner = jnp.where(linked, named // slots, regions + 7)
    slot = named % slots
    every = jnp.arange(slots, dtype=jnp.int32)
    steps = np.array([offset[0] for offset in OFFSETS])
    send_pos = []
    place = {}
    for step in (1, -1):
        rows = np.nonzero(steps == step)[0]
        owns = owner[rows[0] : rows[-1] + 1] == region + step
        sends = jnp.any(owns, axis=0)
        rank = jnp.sum((sends[None, :] & (every[None, :] < every[:, None])).astype(jnp.int32), axis=1)
        send_pos.append(jnp.where(sends, rank, -1))
        there = slot[rows[0] : rows[-1] + 1]
        member = jnp.any(owns[:, :, None] & (there[:, :, None] == every), axis=(0, 1))
        below = jnp.sum(
            (member[None, None, :] & (every < there[:, :, None])).astype(jnp.int32), axis=2
        )
        place[step] = jnp.where(owns, slots + below, -1)
    own = jnp.where(owner == region, slot, -1)
    same = jnp.concatenate([own[9:13], every[None, :], own[13:17]], axis=0)
    left = jnp.where(owner[0:9] == region, slot[0:9], place[-1])
    right = jnp.where(owner[17:26] == region, slot[17:26], place[1])
    first = jnp.where(chan == 0, left, same)
    last = jnp.where(chan == devices - 1, right, same)
    pos = jnp.concatenate([first, same, last], axis=0)
    hot = (pos[:, :, None] == jnp.arange(slots + REACH, dtype=jnp.int32)).astype(BF16)
    return jnp.stack(send_pos), hot


def send_faces(faces, regions, devices):
    got = []
    for flip in range(devices):
        other = (devices - 1) ^ flip
        pairs = [(r * devices + flip, (r + 1) * devices) for r in range(regions - 1)]
        pairs += [(r * devices + other, r * devices - 1) for r in range(1, regions)]
        got.append(lax.ppermute(faces[flip], ("region", "chan"), pairs))
    return got


def swap(value, flip, devices):
    return lax.ppermute(value, "chan", [(source, source ^ flip) for source in range(devices)])


def body(point_feats, destination, voxel_slot, adjacency, active_count, conv_weight, down_weight):
    regions = lax.axis_size("region")
    region = lax.axis_index("region")
    devices = lax.axis_size("chan")
    chan = lax.axis_index("chan")
    me = chan.reshape(1)
    slots = adjacency.shape[0]
    points = point_feats.shape[1]
    cells = slots * 512

    slot = voxel_slot // 512
    inside = voxel_slot % 512
    code = ((inside // 8) * slots + slot) * 8 + inside % 8
    keys, order = lax.sort(
        (destination * cells + code, jnp.arange(points, dtype=jnp.int32)), num_keys=1, is_stable=False
    )
    square = (points // LANES, LANES)
    taps = conv_weight.transpose(2, 3, 4, 0, 1).reshape(27, conv_weight.shape[0], -1)
    down = down_weight.transpose(1, 2, 3, 4, 0).reshape(-1, down_weight.shape[0])
    chunks, middle = exchange(
        point_feats, order.reshape(square), keys.reshape(square), region, regions, cells
    )
    mine = pack(taps, down, middle)
    late = mine[16, 0, 128] != 0
    theirs = [swap(mine, flip, devices) for flip in (1, 2, 3)]
    even, odd, down = prepare(me, mine, theirs, down_weight.shape[0])
    adjacency = jnp.where(late, 0, adjacency)

    send_pos, hot = links(adjacency, region, regions, chan, devices)
    far = far_voxels(me, chunks, regions, slots, (down, hot, send_pos))
    from_two = swap(far, 2, devices)
    near_three, near_one, near, *faces = near_voxels(me, chunks, regions, far, send_pos, slots)
    from_three = swap(near_three, 3, devices)
    from_one = swap(near_one, 1, devices)
    remote = send_faces(faces, regions, devices)
    sums = even_sums(near, from_two, remote[0::2], hot, even)
    coarse = convolve(me, active_count, from_one, from_three, remote[1::2], hot, odd, down, sums)
    back = [swap(coarse[flip], flip, devices) for flip in (1, 2, 3)]
    return finish(me, coarse[0], back, slots)


def solution(mesh):
    return jax.shard_map(
        body,
        mesh=mesh,
        in_specs=(
            P("chan", "region"),
            P("region"),
            P("region"),
            P("region", None),
            P("region"),
            P("chan", None, None, None, None),
            P(None, "chan", None, None, None),
        ),
        out_specs=P("region", "chan"),
        check_vma=False,
    )
```

time: 98.3 us -> 88.6 us (0.901)
  waiting for transfers between devices: 23.9 us -> 9.7 us
  starting transfers between devices: 19.9 us -> 30 us
  Pallas kernels: 38.5 us -> 35.8 us
  local copies, waits for them, and re-layouts: 3.85 us -> 1.83 us
  other arithmetic: 10.7 us -> 9.34 us
    all_to_all x1 -> x0, waiting for transfers between devices: 15.3 us -> none  [body(): moved = lax.all_to_all(moved, 'region', 0, 0, tiled=True)]
    ppermute x4 -> x11, starting transfers between devices: 5.55 us -> 18.8 us  [the longest x7 12.6 us: send(): lax.ppermute(value, 'region', pair)]
    all_to_all x1 -> x0, starting transfers between devices: 6.27 us -> none  [body(): moved = lax.all_to_all(moved, 'region', 0, 0, tiled=True)]
    ppermute x9, starting transfers between devices: 8.08 us -> 11.2 us  [swap(): lax.ppermute(value, 'chan', [(source, source ^ flip) for source in range(...]
    pallas_call x5 -> x10, Pallas kernels: 36.6 us -> 33.9 us  [the longest x4 9.4 us: permute_piece(): pl.pallas_call(functools.partial(piece_kernel, depth, cells, flips), out_...]
    ppermute x4 -> x11, waiting for transfers between devices: 0.01 us -> 2.18 us  [the longest x7 1.92 us: send(): lax.ppermute(value, 'region', pair)]
    reshape x3 -> x0, local copies, waits for them, and re-layouts: 1.38 us -> none  [the longest x2 1.23 us: body(): down_weight.transpose(0, 2, 3, 4, 1).reshape(-1, conv_weight.shape[0], 128)]
    ppermute x9, waiting for transfers between devices: 8.58 us -> 7.52 us  [swap(): lax.ppermute(value, 'chan', [(source, source ^ flip) for source in range(...]
  transfers between devices with their start and end apart: 14 -> 20, of which waited for: 4 -> 5; matrix products, arithmetic and copies ran while one was open for 12% -> 3% of each run, Pallas kernels for 30% -> 24%
where the time goes in v3:
time: 88.6 us; the launch traced here: 88.3 us
  Pallas kernels  35.8 us (40%)
  starting transfers between devices  30 us (34%)
  waiting for transfers between devices  9.7 us (11%)
  other arithmetic  9.34 us (11%)
  local copies, waits for them, and re-layouts  1.83 us (2%)
  between operations  1.6 us (2%)
    ppermute x7, starting transfers between devices, send(): lax.ppermute(value, 'region', pair)  12.6 us
    ppermute x9, starting transfers between devices, swap(): lax.ppermute(value, 'chan', [(source, source ^ flip) for source in range(...  11.2 us
    pallas_call x4, Pallas kernels, permute_piece(): pl.pallas_call(functools.partial(piece_kernel, depth, cells, flips), out_...  9.4 us
    ppermute x9, waiting for transfers between devices, swap(): lax.ppermute(value, 'chan', [(source, source ^ flip) for source in range(...  7.52 us
    pallas_call x1, Pallas kernels, near_voxels(): pl.pallas_call(functools.partial(near_kernel, slots, len(chunks)), out_sh...  6.49 us
    sort x1, other arithmetic, body(): lax.sort((destination * cells + code, jnp.arange(points, dtype=jnp.int32)...  6.45 us
    ppermute x4, starting transfers between devices, send_faces(): got.append(lax.ppermute(faces[flip], ('region', 'chan'), pairs))  6.21 us
    pallas_call x1, Pallas kernels, far_voxels(): pl.pallas_call(functools.partial(far_kernel, len(chunks)), out_shape=jax....  6.08 us
  transfers between devices with their start and end apart: 20, of which 5 were waited for; matrix products, arithmetic and copies ran while one was open for 3% of the time, Pallas kernels for 24%

profile of v3, /device:TPU:0, one launch (start us, length us, event | category | flops | bytes accessed | tf_op | source)
XLA Modules:
  0.0 88.3 jit_solution(15304872893466893917)
XLA Ops:
  0.0 1.0 %fusion.11 = s32[16384]{0:T(1024)S(1)} fusion(s32[16384]{0:T(1024)} %param.11, s32[16384]{0:T(1024)} %param.12), kind=kLoop, calls=%fused_computation.28 | loop fusion | flops 720896 | bytes 196608 | tf_op jit(solution)/shard_map/add | solution.py:619
  1.0 6.4 %sort.15 = (s32[16384]{0:T(1024)S(1)}, s32[16384]{0:T(1024)S(1)}) sort(s32[16384]{0:T(1024)S(1)} %fusion.11, s32[16384]{0:T(1024)S(1)} %iota.21), dimensions={0}, to_apply=%region_0.1 | sort | flops 229376 | bytes 262144 | tf_op jit(solution)/shard_map/sort | solution.py:618
  7.5 0.0 copy-start.2
  7.5 1.0 %copy-done.2 = bf16[16,16384]{1,0:T(8,128)(2,1)S(1)} copy-done((bf16[16,16384]{1,0:T(8,128)(2,1)S(1)}, bf16[16,16384]{1,0:T(8,128)(2,1)}, u32[]{:S(2)}) %copy-start.2) | copy-done | bytes 524312
  8.5 2.3 %permute_piece.5 = (bf16[18,16,128]{2,1,0:T(8,128)(2,1)S(1)}, bf16[18,16,128]{2,1,0:T(8,128)(2,1)S(1)}) custom-call(s32[1]{0:T(128)} %bitcast.1.region, bf16[16,16384]{1,0:T(8,128)(2,1)S(1)} %copy-done.2, s32[128,128]{1,0:T(8,128)S(1)} %bitcast.52, s32[128,128]{1,0:T(8,128)S(1)} %bitcast.48), custom_call_target="tpu_custom_call" | custom-call | flops 2000000000 | bytes 1000000 | tf_op jit(solution)/shard_map/permute_piece/pallas_call | solution.py:126
  10.9 0.1 pack.1.own
  11.0 0.5 collective-permute-start.7
  11.5 2.6 %collective-permute-start.8 = (bf16[17,16,192]{2,1,0:T(8,128)(2,1)S(1)}, bf16[17,16,192]{2,1,0:T(8,128)(2,1)S(1)}, u32[]{:S(2)}, u32[]{:S(2)}) collective-permute-start(bf16[17,16,192]{2,1,0:T(8,128)(2,1)S(1)} %pack.1.own), channel_id=1, source_target_pairs={{0,2},{1,3},{2,0},{3,1},{4,6},{5,7},{6,4},{7,5},{8,10},{9,11},{10,... | collective-permute-start | bytes 313352 | tf_op jit(solution)/shard_map/ppermute | solution.py:602
  14.1 0.1 collective-permute-start.9
  14.2 2.8 %collective-permute-start.2 = (bf16[18,16,128]{2,1,0:T(8,128)(2,1)S(1)}, bf16[18,16,128]{2,1,0:T(8,128)(2,1)S(1)}, u32[]{:S(2)}, u32[]{:S(2)}) collective-permute-start(bf16[18,16,128]{2,1,0:T(8,128)(2,1)S(1)} %get-tuple-element.33._), channel_id=1, source_target_pairs={{0,16},{4,20},{8,24},{12,28},{16,0},{20,4},{24,8},{28,12},{1,17},{... | collective-permute-start | bytes 221192 | tf_op jit(solution)/shard_map/ppermute | solution.py:146
  17.0 1.3 %collective-permute-start.3 = (bf16[18,16,128]{2,1,0:T(8,128)(2,1)S(1)}, bf16[18,16,128]{2,1,0:T(8,128)(2,1)S(1)}, u32[]{:S(2)}, u32[]{:S(2)}) collective-permute-start(bf16[18,16,128]{2,1,0:T(8,128)(2,1)S(1)} %get-tuple-element.34), channel_id=1, source_target_pairs={{0,20},{4,16},{8,28},{12,24},{16,4},{20,0},{24,12},{28,8},{1,21},{... | collective-permute-start | bytes 221192 | tf_op jit(solution)/shard_map/ppermute | solution.py:146
  18.2 0.5 slice.32
  18.7 2.3 %permute_piece.4 = (bf16[18,16,128]{2,1,0:T(8,128)(2,1)S(1)}, bf16[18,16,128]{2,1,0:T(8,128)(2,1)S(1)}) custom-call(s32[1]{0:T(128)} %bitcast.1.region, bf16[16,16384]{1,0:T(8,128)(2,1)S(1)} %copy-done.2, s32[128,128]{1,0:T(8,128)S(1)} %bitcast.53, s32[128,128]{1,0:T(8,128)S(1)} %bitcast.49), custom_call_target="tpu_custom_call" | custom-call | flops 2000000000 | bytes 1000000 | tf_op jit(solution)/shard_map/permute_piece/pallas_call | solution.py:126
  21.7 0.7 fusion.2
  22.4 0.4 convert_reduce_fusion
  22.8 0.4 convert_reduce_fusion.1
  23.2 0.2 concatenate.8
  23.5 0.3 fusion.rest_9_.hot
  23.8 0.1 convert_reduce_fusion.2
  23.9 0.0 collective-permute-done.2.rest_0_.rest_2_
  23.9 3.7 %collective-permute-start = (bf16[18,16,128]{2,1,0:T(8,128)(2,1)S(1)}, bf16[18,16,128]{2,1,0:T(8,128)(2,1)S(1)}, u32[]{:S(2)}, u32[]{:S(2)}) collective-permute-start(bf16[18,16,128]{2,1,0:T(8,128)(2,1)S(1)} %get-tuple-element.31), channel_id=1, source_target_pairs={{0,24},{4,28},{8,16},{12,20},{16,8},{20,12},{24,0},{28,4},{1,25},{... | collective-permute-start | bytes 221192 | tf_op jit(solution)/shard_map/ppermute | solution.py:146
  27.6 0.0 collective-permute-done.3.rest_1_.rest_3_
  27.6 1.3 %collective-permute-start.1 = (bf16[18,16,128]{2,1,0:T(8,128)(2,1)S(1)}, bf16[18,16,128]{2,1,0:T(8,128)(2,1)S(1)}, u32[]{:S(2)}, u32[]{:S(2)}) collective-permute-start(bf16[18,16,128]{2,1,0:T(8,128)(2,1)S(1)} %get-tuple-element.32), channel_id=1, source_target_pairs={{0,28},{4,24},{8,20},{12,16},{16,12},{20,8},{24,4},{28,0},{1,29},{... | collective-permute-start | bytes 221192 | tf_op jit(solution)/shard_map/ppermute | solution.py:146
  28.9 2.4 %permute_piece.7 = (bf16[18,16,128]{2,1,0:T(8,128)(2,1)S(1)}, bf16[18,16,128]{2,1,0:T(8,128)(2,1)S(1)}) custom-call(s32[1]{0:T(128)} %bitcast.1.region, bf16[16,16384]{1,0:T(8,128)(2,1)S(1)} %copy-done.3, s32[128,128]{1,0:T(8,128)S(1)} %bitcast.54, s32[128,128]{1,0:T(8,128)S(1)} %bitcast.50, bf16[18,16,128]{2,1,0:T(8,128)(2,1)S(1)} %collective-permute-done.2.rest_0_.rest_2_, ...), custom_call_target="tpu_custom_call" | custom-call | flops 2000000000 | bytes 1000000 | tf_op jit(solution)/shard_map/permute_piece/pallas_call | solution.py:126
  31.3 0.0 collective-permute-done.rest_0_
  31.3 0.0 copy-start.4
  31.3 1.6 %collective-permute-start.6 = (bf16[18,16,128]{2,1,0:T(8,128)(2,1)S(1)}, bf16[18,16,128]{2,1,0:T(8,128)(2,1)S(1)}, u32[]{:S(2)}, u32[]{:S(2)}) collective-permute-start(bf16[18,16,128]{2,1,0:T(8,128)(2,1)S(1)} %get-tuple-element.37), channel_id=1, source_target_pairs={{0,4},{4,0},{8,12},{12,8},{16,20},{20,16},{24,28},{28,24},{1,5},{5... | collective-permute-start | bytes 221192 | tf_op jit(solution)/shard_map/ppermute | solution.py:146
  32.9 1.9 %collective-permute-done.1.rest_1_ = bf16[18,16,128]{2,1,0:T(8,128)(2,1)S(1)} collective-permute-done((bf16[18,16,128]{2,1,0:T(8,128)(2,1)S(1)}, bf16[18,16,128]{2,1,0:T(8,128)(2,1)S(1)}, u32[]{:S(2)}, u32[]{:S(2)}) %collective-permute-start.1) | collective-permute-done | bytes 73760 | tf_op jit(solution)/shard_map/ppermute | solution.py:146
  34.8 2.3 %permute_piece.6 = (bf16[18,16,128]{2,1,0:T(8,128)(2,1)S(1)}, bf16[18,16,128]{2,1,0:T(8,128)(2,1)S(1)}) custom-call(s32[1]{0:T(128)} %bitcast.1.region, bf16[16,16384]{1,0:T(8,128)(2,1)S(1)} %copy-done.3, s32[128,128]{1,0:T(8,128)S(1)} %bitcast.55, s32[128,128]{1,0:T(8,128)S(1)} %bitcast.51, bf16[18,16,128]{2,1,0:T(8,128)(2,1)S(1)} %collective-permute-done.rest_0_, ...), custom_call_target="tpu_custom_call" | custom-call | flops 2000000000 | bytes 1000000 | tf_op jit(solution)/shard_map/permute_piece/pallas_call | solution.py:126
  37.1 0.1 collective-permute-start.4
  37.2 0.0 collective-permute-done.7.one
  37.2 1.9 %collective-permute-start.5 = (bf16[18,16,128]{2,1,0:T(8,128)(2,1)S(1)}, bf16[18,16,128]{2,1,0:T(8,128)(2,1)S(1)}, u32[]{:S(2)}, u32[]{:S(2)}) collective-permute-start(bf16[18,16,128]{2,1,0:T(8,128)(2,1)S(1)} %get-tuple-element.36), channel_id=1, source_target_pairs={{0,12},{4,8},{8,4},{12,0},{16,28},{20,24},{24,20},{28,16},{1,13},{... | collective-permute-start | bytes 221192 | tf_op jit(solution)/shard_map/ppermute | solution.py:146
  39.1 0.0 collective-permute-done.8.two
  39.1 0.0 collective-permute-done.9.three
  39.1 3.6 %prepare.1 = (bf16[2,9,256,256]{3,2,1,0:T(8,128)(2,1)S(1)}, bf16[2,9,256,256]{3,2,1,0:T(8,128)(2,1)S(1)}, bf16[128,512]{1,0:T(8,128)(2,1)S(1)}) custom-call(s32[1]{0:T(128)} %bitcast.chan, bf16[4,384,192]{2,1,0:T(8,128)(2,1)S(1)} %copy-done.4, bf16[17,16,192]{2,1,0:T(8,128)(2,1)S(1)} %pack.1.own, bf16[17,16,192]{2,1,0:T(8,128)(2,1)S(1)} %collective-permute-done.7.one, ...), custom_call_target="tpu_custom_call" | custom-call | flops 2000000000 | bytes 3000000 | tf_op jit(solution)/shard_map/prepare/pallas_call | solution.py:398
  42.7 0.0 collective-permute-done.6.rest_6_
  42.7 0.0 collective-permute-done.4.rest_4_
  42.7 0.0 collective-permute-done.5.rest_5_
  42.7 6.1 %far_voxels.1.rest_8_ = bf16[4,512,128]{2,1,0:T(8,128)(2,1)S(1)} custom-call(s32[1]{0:T(128)} %bitcast.chan, bf16[18,16,128]{2,1,0:T(8,128)(2,1)S(1)} %collective-permute-done.rest_0_, bf16[18,16,128]{2,1,0:T(8,128)(2,1)S(1)} %collective-permute-done.1.rest_1_, bf16[18,16,128]{2,1,0:T(8,128)(2,1)S(1)} %collective-permute-done.2.rest_0_.rest_2_, ...), custom_call_target="tpu_custom_call" | custom-call | flops 4000000000 | bytes 1200000 | tf_op jit(solution)/shard_map/far_voxels/pallas_call | solution.py:301
  48.8 0.0 copy-start.5
  48.8 2.0 %collective-permute-start.14 = (bf16[4,512,128]{2,1,0:T(8,128)(2,1)S(1)}, bf16[4,512,128]{2,1,0:T(8,128)(2,1)S(1)}, u32[]{:S(2)}, u32[]{:S(2)}) collective-permute-start(bf16[4,512,128]{2,1,0:T(8,128)(2,1)S(1)} %far_voxels.1.rest_8_), channel_id=1, source_target_pairs={{0,2},{1,3},{2,0},{3,1},{4,6},{5,7},{6,4},{7,5},{8,10},{9,11},{10,... | collective-permute-start | bytes 1572872 | tf_op jit(solution)/shard_map/ppermute | solution.py:602
  50.8 6.5 %near_voxels.1 = (bf16[4,512,128]{2,1,0:T(8,128)(2,1)S(1)}, bf16[4,512,128]{2,1,0:T(8,128)(2,1)S(1)}, bf16[4,512,128]{2,1,0:T(8,128)(2,1)S(1)}, bf16[8,16,128]{2...) custom-call(s32[1]{0:T(128)} %bitcast.chan, ...), custom_call_target="tpu_custom_call" | custom-call | flops 4000000000 | bytes 3000000 | tf_op jit(solution)/shard_map/near_voxels/pallas_call | solution.py:314
  57.3 0.1 collective-permute-start.10
  57.4 0.1 collective-permute-start.11
  57.5 4.0 %collective-permute-start.15 = (bf16[8,16,128]{2,1,0:T(8,128)(2,1)S(1)}, bf16[8,16,128]{2,1,0:T(8,128)(2,1)S(1)}, u32[]{:S(2)}, u32[]{:S(2)}) collective-permute-start(bf16[8,16,128]{2,1,0:T(8,128)(2,1)S(1)} %get-tuple-element.46), channel_id=1, source_target_pairs={{0,4},{4,8},{8,12},{12,16},{16,20},{20,24},{24,28},{7,3},{11,7},{1... | collective-permute-start | bytes 98312 | tf_op jit(solution)/shard_map/ppermute | solution.py:597
  61.4 0.7 collective-permute-start.16
  62.8 0.3 collective-permute-done.15.r0
  63.0 0.7 collective-permute-start.12
  63.7 0.0 collective-permute-done.16.r2
  63.7 0.9 %collective-permute-start.13 = (bf16[8,16,128]{2,1,0:T(8,128)(2,1)S(1)}, bf16[8,16,128]{2,1,0:T(8,128)(2,1)S(1)}, u32[]{:S(2)}, u32[]{:S(2)}) collective-permute-start(bf16[8,16,128]{2,1,0:T(8,128)(2,1)S(1)} %get-tuple-element.43), channel_id=1, source_target_pairs={{3,4},{7,8},{11,12},{15,16},{19,20},{23,24},{27,28},{4,3},{8,7},{1... | collective-permute-start | bytes 98312 | tf_op jit(solution)/shard_map/ppermute | solution.py:597
  64.6 0.0 collective-permute-done.14.two
  64.6 3.9 %even_sums.1.sums = f32[2,2,512,256]{3,2,1,0:T(8,128)S(1)} custom-call(bf16[4,512,128]{2,1,0:T(8,128)(2,1)S(1)} %get-tuple-element.45.own, bf16[4,512,128]{2,1,0:T(8,128)(2,1)S(1)} %collective-permute-done.14.two, bf16[8,16,128]{2,1,0:T(8,128)(2,1)S(1)} %collective-permute-done.15.r0, bf16[8,16,128]{2,1,0:T(8,128)(2,1)S(1)} %collective-permute-done.16.r2, ...), custom_call_target="tpu_custom_call" | custom-call | flops 4000000000 | bytes 5000000 | tf_op jit(solution)/shard_map/even_sums/pallas_call | solution.py:497
  68.6 0.0 collective-permute-done.12.r1
  68.6 0.0 collective-permute-done.13.r3
  68.6 0.0 collective-permute-done.10.one
  68.6 3.1 %collective-permute-done.11.three = bf16[4,512,128]{2,1,0:T(8,128)(2,1)S(1)} collective-permute-done((bf16[4,512,128]{2,1,0:T(8,128)(2,1)S(1)}, bf16[4,512,128]{2,1,0:T(8,128)(2,1)S(1)}, u32[]{:S(2)}, u32[]{:S(2)}) %collective-permute-start.11) | collective-permute-done | bytes 524320 | tf_op jit(solution)/shard_map/ppermute | solution.py:602
  71.7 4.3 %convolve.1 = (bf16[32,1024]{1,0:T(8,128)(2,1)S(1)}, bf16[32,1024]{1,0:T(8,128)(2,1)S(1)}, bf16[32,1024]{1,0:T(8,128)(2,1)S(1)}, bf16[32,1024]{1,0:T(8,128)(2,1)S(1)}) custom-call(s32[1]{0:T(128)} %bitcast.chan, s32[1]{0:T(128)S(6)} %copy.11.active, bf16[4,512,128]{2,1,0:T(8,128)(2,1)S(1)} %collective-permute-done.10.one, ...), custom_call_target="tpu_custom_call" | custom-call | flops 4000000000 | bytes 5000000 | tf_op jit(solution)/shard_map/convolve/pallas_call | solution.py:516
  76.1 0.6 collective-permute-start.17
  76.7 5.3 %collective-permute-start.18 = (bf16[32,1024]{1,0:T(8,128)(2,1)S(1)}, bf16[32,1024]{1,0:T(8,128)(2,1)S(1)}, u32[]{:S(2)}, u32[]{:S(2)}) collective-permute-start(bf16[32,1024]{1,0:T(8,128)(2,1)S(1)} %get-tuple-element.51), channel_id=1, source_target_pairs={{0,2},{1,3},{2,0},{3,1},{4,6},{5,7},{6,4},{7,5},{8,10},{9,11},{10,... | collective-permute-start | bytes 196616 | tf_op jit(solution)/shard_map/ppermute | solution.py:602
  82.0 0.0 collective-permute-start.19
  82.0 0.0 collective-permute-done.17.one
  82.0 2.3 %collective-permute-done.18.two = bf16[32,1024]{1,0:T(8,128)(2,1)S(1)} collective-permute-done((bf16[32,1024]{1,0:T(8,128)(2,1)S(1)}, bf16[32,1024]{1,0:T(8,128)(2,1)S(1)}, u32[]{:S(2)}, u32[]{:S(2)}) %collective-permute-start.18) | collective-permute-done | bytes 65568 | tf_op jit(solution)/shard_map/ppermute | solution.py:602
  84.4 2.0 %collective-permute-done.19.three = bf16[32,1024]{1,0:T(8,128)(2,1)S(1)} collective-permute-done((bf16[32,1024]{1,0:T(8,128)(2,1)S(1)}, bf16[32,1024]{1,0:T(8,128)(2,1)S(1)}, u32[]{:S(2)}, u32[]{:S(2)}) %collective-permute-start.19) | collective-permute-done | bytes 65568 | tf_op jit(solution)/shard_map/ppermute | solution.py:602
  86.4 1.9 %finish.1 = bf16[64,2048]{1,0:T(8,128)(2,1)} custom-call(s32[1]{0:T(128)} %bitcast.chan, bf16[32,1024]{1,0:T(8,128)(2,1)S(1)} %get-tuple-element.49.own, bf16[32,1024]{1,0:T(8,128)(2,1)S(1)} %collective-permute-done.17.one, bf16[32,1024]{1,0:T(8,128)(2,1)S(1)} %collective-permute-done.18.two, bf16[32,1024]{1,0:T(8,128)(2,1)S(1)} %collective-permute-done.19.three), custom_call_target="tpu_custom_call" | custom-call | tf_op jit(solution)/shard_map/finish/pallas_call | solution.py:547
  (21 shorter events, 0.1 us)
Async XLA Ops:
  7.5 1.0 %copy-start.2 = (bf16[16,16384]{1,0:T(8,128)(2,1)S(1)}, bf16[16,16384]{1,0:T(8,128)(2,1)}, u32[]{:S(2)}) copy-start(bf16[16,16384]{1,0:T(8,128)(2,1)} %feats.7) | copy-start | bytes 1572868
  8.5 2.4 %copy-start = (bf16[16,64,3,3,3]{1,0,4,3,2:T(8,128)(2,1)S(1)}, bf16[16,64,3,3,3]{1,0,4,3,2:T(8,128)(2,1)}, u32[]{:S(2)}) copy-start(bf16[16,64,3,3,3]{1,0,4,3,2:T(8,128)(2,1)} %param.15) | copy-start | bytes 165892
  8.5 2.4 %copy-start.1 = (bf16[128,16,2,2,2]{0,4,3,2,1:T(2,128)(2,1)S(1)}, bf16[128,16,2,2,2]{0,4,3,2,1:T(2,128)(2,1)}, u32[]{:S(2)}) copy-start(bf16[128,16,2,2,2]{0,4,3,2,1:T(2,128)(2,1)} %param.16) | copy-start | bytes 98308
  11.0 26.2 %collective-permute-start.7 = (bf16[17,16,192]{2,1,0:T(8,128)(2,1)S(1)}, bf16[17,16,192]{2,1,0:T(8,128)(2,1)S(1)}, u32[]{:S(2)}, u32[]{:S(2)}) collective-permute-start(bf16[17,16,192]{2,1,0:T(8,128)(2,1)S(1)} %pack.1.own), channel_id=1, source_target_pairs={{0,1},{1,0},{2,3},{3,2},{4,5},{5,4},{6,7},{7,6},{8,9},{9,8},{10,11... | collective-permute-start | bytes 313352 | tf_op jit(solution)/shard_map/ppermute | solution.py:602
  11.5 27.6 %collective-permute-start.8 = (bf16[17,16,192]{2,1,0:T(8,128)(2,1)S(1)}, bf16[17,16,192]{2,1,0:T(8,128)(2,1)S(1)}, u32[]{:S(2)}, u32[]{:S(2)}) collective-permute-start(bf16[17,16,192]{2,1,0:T(8,128)(2,1)S(1)} %pack.1.own), channel_id=1, source_target_pairs={{0,2},{1,3},{2,0},{3,1},{4,6},{5,7},{6,4},{7,5},{8,10},{9,11},{10,... | collective-permute-start | bytes 313352 | tf_op jit(solution)/shard_map/ppermute | solution.py:602
  14.1 25.0 %collective-permute-start.9 = (bf16[17,16,192]{2,1,0:T(8,128)(2,1)S(1)}, bf16[17,16,192]{2,1,0:T(8,128)(2,1)S(1)}, u32[]{:S(2)}, u32[]{:S(2)}) collective-permute-start(bf16[17,16,192]{2,1,0:T(8,128)(2,1)S(1)} %pack.1.own), channel_id=1, source_target_pairs={{0,3},{1,2},{2,1},{3,0},{4,7},{5,6},{6,5},{7,4},{8,11},{9,10},{10,... | collective-permute-start | bytes 313352 | tf_op jit(solution)/shard_map/ppermute | solution.py:602
  14.2 9.8 %collective-permute-start.2 = (bf16[18,16,128]{2,1,0:T(8,128)(2,1)S(1)}, bf16[18,16,128]{2,1,0:T(8,128)(2,1)S(1)}, u32[]{:S(2)}, u32[]{:S(2)}) collective-permute-start(bf16[18,16,128]{2,1,0:T(8,128)(2,1)S(1)} %get-tuple-element.33._), channel_id=1, source_target_pairs={{0,16},{4,20},{8,24},{12,28},{16,0},{20,4},{24,8},{28,12},{1,17},{... | collective-permute-start | bytes 221192 | tf_op jit(solution)/shard_map/ppermute | solution.py:146
  17.0 10.6 %collective-permute-start.3 = (bf16[18,16,128]{2,1,0:T(8,128)(2,1)S(1)}, bf16[18,16,128]{2,1,0:T(8,128)(2,1)S(1)}, u32[]{:S(2)}, u32[]{:S(2)}) collective-permute-start(bf16[18,16,128]{2,1,0:T(8,128)(2,1)S(1)} %get-tuple-element.34), channel_id=1, source_target_pairs={{0,20},{4,16},{8,28},{12,24},{16,4},{20,0},{24,12},{28,8},{1,21},{... | collective-permute-start | bytes 221192 | tf_op jit(solution)/shard_map/ppermute | solution.py:146
  18.7 2.9 %copy-start.6 = (s32[64,26]{0,1:T(8,128)S(1)}, s32[64,26]{0,1:T(8,128)}, u32[]{:S(2)}) copy-start(s32[64,26]{0,1:T(8,128)} %param.13) | copy-start | bytes 19972
  18.7 10.2 %copy-start.3 = (bf16[16,16384]{1,0:T(8,128)(2,1)S(1)}, bf16[16,16384]{1,0:T(8,128)(2,1)}, u32[]{:S(2)}) copy-start(bf16[16,16384]{1,0:T(8,128)(2,1)} %feats.7) | copy-start | bytes 1572868
  23.9 7.4 %collective-permute-start = (bf16[18,16,128]{2,1,0:T(8,128)(2,1)S(1)}, bf16[18,16,128]{2,1,0:T(8,128)(2,1)S(1)}, u32[]{:S(2)}, u32[]{:S(2)}) collective-permute-start(bf16[18,16,128]{2,1,0:T(8,128)(2,1)S(1)} %get-tuple-element.31), channel_id=1, source_target_pairs={{0,24},{4,28},{8,16},{12,20},{16,8},{20,12},{24,0},{28,4},{1,25},{... | collective-permute-start | bytes 221192 | tf_op jit(solution)/shard_map/ppermute | solution.py:146
  27.6 7.2 %collective-permute-start.1 = (bf16[18,16,128]{2,1,0:T(8,128)(2,1)S(1)}, bf16[18,16,128]{2,1,0:T(8,128)(2,1)S(1)}, u32[]{:S(2)}, u32[]{:S(2)}) collective-permute-start(bf16[18,16,128]{2,1,0:T(8,128)(2,1)S(1)} %get-tuple-element.32), channel_id=1, source_target_pairs={{0,28},{4,24},{8,20},{12,16},{16,12},{20,8},{24,4},{28,0},{1,29},{... | collective-permute-start | bytes 221192 | tf_op jit(solution)/shard_map/ppermute | solution.py:146
  31.3 7.8 %copy-start.4 = (bf16[4,384,192]{2,1,0:T(8,128)(2,1)S(1)}, bf16[4,384,192]{2,1,0:T(8,128)(2,1)}, u32[]{:S(2)}) copy-start(bf16[4,384,192]{2,1,0:T(8,128)(2,1)} %constant.103.clone.spread) | copy-start | bytes 1769476
  31.3 11.4 %collective-permute-start.6 = (bf16[18,16,128]{2,1,0:T(8,128)(2,1)S(1)}, bf16[18,16,128]{2,1,0:T(8,128)(2,1)S(1)}, u32[]{:S(2)}, u32[]{:S(2)}) collective-permute-start(bf16[18,16,128]{2,1,0:T(8,128)(2,1)S(1)} %get-tuple-element.37), channel_id=1, source_target_pairs={{0,4},{4,0},{8,12},{12,8},{16,20},{20,16},{24,28},{28,24},{1,5},{5... | collective-permute-start | bytes 221192 | tf_op jit(solution)/shard_map/ppermute | solution.py:146
  37.1 5.6 %collective-permute-start.4 = (bf16[18,16,128]{2,1,0:T(8,128)(2,1)S(1)}, bf16[18,16,128]{2,1,0:T(8,128)(2,1)S(1)}, u32[]{:S(2)}, u32[]{:S(2)}) collective-permute-start(bf16[18,16,128]{2,1,0:T(8,128)(2,1)S(1)} %get-tuple-element.35), channel_id=1, source_target_pairs={{0,8},{4,12},{8,0},{12,4},{16,24},{20,28},{24,16},{28,20},{1,9},{5... | collective-permute-start | bytes 221192 | tf_op jit(solution)/shard_map/ppermute | solution.py:146
  37.2 5.5 %collective-permute-start.5 = (bf16[18,16,128]{2,1,0:T(8,128)(2,1)S(1)}, bf16[18,16,128]{2,1,0:T(8,128)(2,1)S(1)}, u32[]{:S(2)}, u32[]{:S(2)}) collective-permute-start(bf16[18,16,128]{2,1,0:T(8,128)(2,1)S(1)} %get-tuple-element.36), channel_id=1, source_target_pairs={{0,12},{4,8},{8,4},{12,0},{16,28},{20,24},{24,20},{28,16},{1,13},{... | collective-permute-start | bytes 221192 | tf_op jit(solution)/shard_map/ppermute | solution.py:146
  48.8 15.8 %copy-start.5 = (bf16[256,128]{1,0:T(8,128)(2,1)S(1)}, bf16[256,128]{1,0:T(8,128)(2,1)}, u32[]{:S(2)}) copy-start(bf16[256,128]{1,0:T(8,128)(2,1)} %constant.104.clone.pick) | copy-start | bytes 196612
  48.8 15.8 %collective-permute-start.14 = (bf16[4,512,128]{2,1,0:T(8,128)(2,1)S(1)}, bf16[4,512,128]{2,1,0:T(8,128)(2,1)S(1)}, u32[]{:S(2)}, u32[]{:S(2)}) collective-permute-start(bf16[4,512,128]{2,1,0:T(8,128)(2,1)S(1)} %far_voxels.1.rest_8_), channel_id=1, source_target_pairs={{0,2},{1,3},{2,0},{3,1},{4,6},{5,7},{6,4},{7,5},{8,10},{9,11},{10,... | collective-permute-start | bytes 1572872 | tf_op jit(solution)/shard_map/ppermute | solution.py:602
  57.3 11.3 %collective-permute-start.10 = (bf16[4,512,128]{2,1,0:T(8,128)(2,1)S(1)}, bf16[4,512,128]{2,1,0:T(8,128)(2,1)S(1)}, u32[]{:S(2)}, u32[]{:S(2)}) collective-permute-start(bf16[4,512,128]{2,1,0:T(8,128)(2,1)S(1)} %get-tuple-element.40), channel_id=1, source_target_pairs={{0,1},{1,0},{2,3},{3,2},{4,5},{5,4},{6,7},{7,6},{8,9},{9,8},{10,11... | collective-permute-start | bytes 1572872 | tf_op jit(solution)/shard_map/ppermute | solution.py:602
  57.4 14.3 %collective-permute-start.11 = (bf16[4,512,128]{2,1,0:T(8,128)(2,1)S(1)}, bf16[4,512,128]{2,1,0:T(8,128)(2,1)S(1)}, u32[]{:S(2)}, u32[]{:S(2)}) collective-permute-start(bf16[4,512,128]{2,1,0:T(8,128)(2,1)S(1)} %get-tuple-element.41), channel_id=1, source_target_pairs={{0,3},{1,2},{2,1},{3,0},{4,7},{5,6},{6,5},{7,4},{8,11},{9,10},{10,... | collective-permute-start | bytes 1572872 | tf_op jit(solution)/shard_map/ppermute | solution.py:602
  57.5 5.6 %collective-permute-start.15 = (bf16[8,16,128]{2,1,0:T(8,128)(2,1)S(1)}, bf16[8,16,128]{2,1,0:T(8,128)(2,1)S(1)}, u32[]{:S(2)}, u32[]{:S(2)}) collective-permute-start(bf16[8,16,128]{2,1,0:T(8,128)(2,1)S(1)} %get-tuple-element.46), channel_id=1, source_target_pairs={{0,4},{4,8},{8,12},{12,16},{16,20},{20,24},{24,28},{7,3},{11,7},{1... | collective-permute-start | bytes 98312 | tf_op jit(solution)/shard_map/ppermute | solution.py:597
  61.4 2.2 %collective-permute-start.16 = (bf16[8,16,128]{2,1,0:T(8,128)(2,1)S(1)}, bf16[8,16,128]{2,1,0:T(8,128)(2,1)S(1)}, u32[]{:S(2)}, u32[]{:S(2)}) collective-permute-start(bf16[8,16,128]{2,1,0:T(8,128)(2,1)S(1)} %get-tuple-element.47), channel_id=1, source_target_pairs={{2,4},{6,8},{10,12},{14,16},{18,20},{22,24},{26,28},{5,3},{9,7},{1... | collective-permute-start | bytes 98312 | tf_op jit(solution)/shard_map/ppermute | solution.py:597
  63.0 5.5 %collective-permute-start.12 = (bf16[8,16,128]{2,1,0:T(8,128)(2,1)S(1)}, bf16[8,16,128]{2,1,0:T(8,128)(2,1)S(1)}, u32[]{:S(2)}, u32[]{:S(2)}) collective-permute-start(bf16[8,16,128]{2,1,0:T(8,128)(2,1)S(1)} %get-tuple-element.42), channel_id=1, source_target_pairs={{1,4},{5,8},{9,12},{13,16},{17,20},{21,24},{25,28},{6,3},{10,7},{1... | collective-permute-start | bytes 98312 | tf_op jit(solution)/shard_map/ppermute | solution.py:597
  63.7 4.9 %collective-permute-start.13 = (bf16[8,16,128]{2,1,0:T(8,128)(2,1)S(1)}, bf16[8,16,128]{2,1,0:T(8,128)(2,1)S(1)}, u32[]{:S(2)}, u32[]{:S(2)}) collective-permute-start(bf16[8,16,128]{2,1,0:T(8,128)(2,1)S(1)} %get-tuple-element.43), channel_id=1, source_target_pairs={{3,4},{7,8},{11,12},{15,16},{19,20},{23,24},{27,28},{4,3},{8,7},{1... | collective-permute-start | bytes 98312 | tf_op jit(solution)/shard_map/ppermute | solution.py:597
  76.1 6.0 %collective-permute-start.17 = (bf16[32,1024]{1,0:T(8,128)(2,1)S(1)}, bf16[32,1024]{1,0:T(8,128)(2,1)S(1)}, u32[]{:S(2)}, u32[]{:S(2)}) collective-permute-start(bf16[32,1024]{1,0:T(8,128)(2,1)S(1)} %get-tuple-element.50), channel_id=1, source_target_pairs={{0,1},{1,0},{2,3},{3,2},{4,5},{5,4},{6,7},{7,6},{8,9},{9,8},{10,11... | collective-permute-start | bytes 196616 | tf_op jit(solution)/shard_map/ppermute | solution.py:602
  76.7 7.7 %collective-permute-start.18 = (bf16[32,1024]{1,0:T(8,128)(2,1)S(1)}, bf16[32,1024]{1,0:T(8,128)(2,1)S(1)}, u32[]{:S(2)}, u32[]{:S(2)}) collective-permute-start(bf16[32,1024]{1,0:T(8,128)(2,1)S(1)} %get-tuple-element.51), channel_id=1, source_target_pairs={{0,2},{1,3},{2,0},{3,1},{4,6},{5,7},{6,4},{7,5},{8,10},{9,11},{10,... | collective-permute-start | bytes 196616 | tf_op jit(solution)/shard_map/ppermute | solution.py:602
  82.0 4.4 %collective-permute-start.19 = (bf16[32,1024]{1,0:T(8,128)(2,1)S(1)}, bf16[32,1024]{1,0:T(8,128)(2,1)S(1)}, u32[]{:S(2)}, u32[]{:S(2)}) collective-permute-start(bf16[32,1024]{1,0:T(8,128)(2,1)S(1)} %get-tuple-element.52), channel_id=1, source_target_pairs={{0,3},{1,2},{2,1},{3,0},{4,7},{5,6},{6,5},{7,4},{8,11},{9,10},{10,... | collective-permute-start | bytes 196616 | tf_op jit(solution)/shard_map/ppermute | solution.py:602
